TPU v7x, 256 devices: a whole 4x4x8 slice. The times are simulated.
256 devices in a mesh: group: 8 (over x_lo, y), shard: 32 (over z, x_hi, core).
Axes of the slice: x: 4 (x_hi: 2, x_lo: 2; x = x_hi * 2 + x_lo), y: 4, z: 8, core: 2. Of those that a mesh axis runs over, the one named last changes fastest.
Arguments:
- weights: bfloat16 [8, 10240, 7168], P('group', 'shard'), may hold values from -64 to 64
- factor_init: float32 [8, 16, 7168], P('group'), may hold values from -6 to 6
Outputs:
- new_weights: bfloat16 [8, 10240, 7168], P('group', 'shard')
- next_factor: float32 [8, 16, 7168], P('group')
All inputs are finite; a program needn't handle non-finite values.
Results may differ from a plain program's by a relative error of at most 0.0051.
Values may be sent and summed in bfloat16 or wider, within the bound.
A program may use at most 64 MiB of HBM per device.

v0:
```python
import jax
import jax.numpy as jnp
from jax import lax
from jax.sharding import PartitionSpec as P

STEPS = 2


gossip_rate = 0.5


def shifted(value, axis, steps):
    count = lax.axis_size(axis)
    pairs = [(source, (source + steps) % count) for source in range(count)]
    return lax.ppermute(value, axis, pairs)


def gram_of(raw_rows):
    return jnp.dot(raw_rows, raw_rows.T, precision=lax.Precision.HIGHEST)


def solve_with(gram_matrix, raw_rows):
    lower = lax.linalg.cholesky(gram_matrix)
    return lax.linalg.triangular_solve(lower, raw_rows, left_side=True, lower=True)


def orthonormal(raw_left, raw_right):
    gram_left, gram_right = lax.psum((gram_of(raw_left), gram_of(raw_right)), "shard")
    return (solve_with(gram_left, raw_left), solve_with(gram_right, raw_right))


def body(weights, factor_init):
    local = weights[0]
    rank = factor_init.shape[1]
    right_factor = factor_init[0]
    left_factor = None
    left_rounded = shifted(factor_init.astype(jnp.bfloat16), "group", 1)[0]
    right_rounded = right_factor.astype(jnp.bfloat16)
    basis_left = None
    basis_right = None
    for repeat in range(STEPS):
        stacked = jnp.concatenate([left_rounded, right_rounded], axis=0)
        own_terms = lax.dot_general(
            stacked, local, (((1,), (1,)), ((), ())), preferred_element_type=jnp.float32
        )
        own_left = own_terms[:rank]
        own_right = own_terms[rank:]
        from_left = shifted(own_right, "group", 1)
        from_right = shifted(own_left, "group", -1)
        basis_left, basis_right = orthonormal(from_left - own_left, own_right - from_right)
        basis_bf = jnp.concatenate([basis_left, basis_right], axis=0).astype(jnp.bfloat16)
        products = jnp.dot(basis_bf, local, preferred_element_type=jnp.float32)
        part_left = products[:rank]
        part_right = products[rank:]
        sum_left, sum_right = lax.psum((part_left, part_right), "shard")
        left_factor = shifted(sum_right, "group", 1) - sum_left
        right_factor = sum_right - shifted(sum_left, "group", -1)
        left_rounded = left_factor.astype(jnp.bfloat16)
        right_rounded = right_factor.astype(jnp.bfloat16)
    signed = jnp.concatenate([-basis_left, basis_right], axis=0)
    factors = jnp.concatenate([left_factor, right_factor], axis=0)
    delta = lax.dot_general(
        signed,
        factors,
        (((0,), (0,)), ((), ())),
        precision=lax.Precision.HIGHEST,
        preferred_element_type=jnp.float32,
    )
    updated = (local.astype(jnp.float32) - gossip_rate * delta).astype(jnp.bfloat16)
    return (updated[None], right_factor[None])


def solution(mesh):
    in_specs = (P("group", "shard", None), P("group", None, None))
    out_specs = (P("group", "shard", None), P("group", None, None))
    return jax.shard_map(body, mesh=mesh, in_specs=in_specs, out_specs=out_specs, check_vma=False)
```

profile of v0, /device:TPU:1, one launch (start us, length us, event | category | flops | bytes accessed | tf_op | source)
XLA Modules:
  0.0 901.1 jit_solution(12994734388459710599)
XLA Ops:
  8.3 2.2 collective-permute-start
  11.5 4.7 collective-permute-done
  16.2 3.7 fusion.9
  20.5 3.1 collective-permute-start.2
  23.6 1.2 collective-permute-done.1
  25.2 132.4 %all-reduce.1 = (f32[16,16]{0,1:T(8,128)S(1)}, f32[16,16]{0,1:T(8,128)S(1)}) all-reduce(f32[16,16]{0,1:T(8,128)S(1)} %fusion.55, f32[16,16]{0,1:T(8,128)S(1)} %fusion.54), channel_id=1, replica_groups=mesh['group'=8,'shard'=32] {'shard'}, use_global_device_ids=true, to_apply=%region_3.6 | all-reduce | flops 512 | bytes 4096 | tf_op jit(solution)/shard_map/psum | solution.py:28
  157.7 1.5 custom-call.14
  160.5 1.2 custom-call.15
  161.8 1.5 custom-call.12
  164.6 1.2 custom-call.13
  166.3 3.2 fusion.7
  170.5 264.8 %all-reduce.9.cloned.1.call-done = (f32[16,7168]{1,0:T(8,128)}, f32[16,7168]{1,0:T(8,128)}) async-done(((f32[16,7168]{1,0:T(8,128)}, f32[16,7168]{1,0:T(8,128)}), (f32[16,7168]{1,0:T(8,128)}, f32[16,7168]{1,0:T(8,128)})) %all-reduce.9.cloned.1.call-update) | async-done | bytes 917520 | tf_op jit(solution)/shard_map/psum | solution.py:55
  435.3 1.2 collective-permute-start.3
  436.5 2.4 collective-permute-start.4
  438.9 8.3 collective-permute-done.3
  448.2 1.1 subtract_convert_fusion
  449.3 3.7 fusion.5
  453.2 3.6 collective-permute-start.6
  456.7 1.2 collective-permute-done.5
  458.3 129.4 %all-reduce = (f32[16,16]{0,1:T(8,128)S(1)}, f32[16,16]{0,1:T(8,128)S(1)}) all-reduce(f32[16,16]{0,1:T(8,128)S(1)} %fusion.53, f32[16,16]{0,1:T(8,128)S(1)} %fusion.52), channel_id=1, replica_groups=mesh['group'=8,'shard'=32] {'shard'}, use_global_device_ids=true, to_apply=%region_7.10 | all-reduce | flops 512 | bytes 4096 | tf_op jit(solution)/shard_map/psum | solution.py:28
  587.7 1.5 custom-call.18
  590.5 1.2 custom-call.19
  591.8 1.5 custom-call.16
  594.6 1.2 custom-call.17
  596.3 3.2 fusion.3
  600.5 268.6 %all-reduce.7.cloned.1.call-done = (f32[16,7168]{1,0:T(8,128)}, f32[16,7168]{1,0:T(8,128)}) async-done(((f32[16,7168]{1,0:T(8,128)}, f32[16,7168]{1,0:T(8,128)}), (f32[16,7168]{1,0:T(8,128)}, f32[16,7168]{1,0:T(8,128)})) %all-reduce.7.cloned.1.call-update) | async-done | bytes 917520 | tf_op jit(solution)/shard_map/psum | solution.py:55
  869.1 1.2 collective-permute-start.7
  870.3 2.4 collective-permute-start.8
  872.7 8.3 collective-permute-done.7
  881.0 1.1 sub.33
  882.1 1.1 sub.34
  883.2 11.1 %fusion.2 = bf16[1,320,7168]{2,1,0:T(8,128)(2,1)} fusion(bf16[1,320,7168]{2,1,0:T(8,128)(2,1)} %param.5, f32[16,7168]{1,0:T(8,128)S(1)} %sub.34, f32[16,7168]{1,0:T(8,128)S(1)} %sub.33, f32[16,320]{1,0:T(8,128)S(1)} %get-tuple-element.23, f32[16,320]{1,0:T(8,128)S(1)} %get-tuple-element.20), kind=kOutput, calls=%fused_computation.3 | convolution fusion | flops 890218496 | bytes 10133504 | tf_op jit(solution)/shard_map/dot_general | solution.py:62
  (46 shorter events, 13.2 us)
Async XLA Ops:
  7.2 428.1 %all-reduce.9.cloned.1.call-start = ((), (), s32[]{:S(2)}) async-start(), calls=%async_computation.1 | async-start | bytes 1835008 | tf_op jit(solution)/shard_map/psum | solution.py:55
  8.3 8.0 collective-permute-start
  20.0 4.9 collective-permute-start.1
  20.5 4.4 collective-permute-start.2
  170.5 698.7 %all-reduce.7.cloned.1.call-start = ((), (), s32[]{:S(2)}) async-start(), calls=%async_computation | async-start | bytes 1835008 | tf_op jit(solution)/shard_map/psum | solution.py:55
  435.3 11.9 %collective-permute-start.3 = (f32[16,7168]{1,0:T(8,128)}, f32[16,7168]{1,0:T(8,128)S(1)}, u32[]{:S(2)}, u32[]{:S(2)}) collective-permute-start(f32[16,7168]{1,0:T(8,128)} %get-tuple-element.10), channel_id=1, source_target_pairs={{0,32},{32,64},{64,96},{96,128},{128,160},{160,192},{192,224},{224... | collective-permute-start | bytes 1376264 | tf_op jit(solution)/shard_map/ppermute | solution.py:15
  436.5 11.7 %collective-permute-start.4 = (f32[16,7168]{1,0:T(8,128)}, f32[16,7168]{1,0:T(8,128)S(1)}, u32[]{:S(2)}, u32[]{:S(2)}) collective-permute-start(f32[16,7168]{1,0:T(8,128)} %get-tuple-element.11), channel_id=1, source_target_pairs={{0,224},{32,0},{64,32},{96,64},{128,96},{160,128},{192,160},{224,1... | collective-permute-start | bytes 1376264 | tf_op jit(solution)/shard_map/ppermute | solution.py:15
  453.1 4.9 collective-permute-start.5
  453.2 4.9 collective-permute-start.6
  869.1 11.9 %collective-permute-start.7 = (f32[16,7168]{1,0:T(8,128)}, f32[16,7168]{1,0:T(8,128)S(1)}, u32[]{:S(2)}, u32[]{:S(2)}) collective-permute-start(f32[16,7168]{1,0:T(8,128)} %get-tuple-element.8), channel_id=1, source_target_pairs={{0,32},{32,64},{64,96},{96,128},{128,160},{160,192},{192,224},{224... | collective-permute-start | bytes 1376264 | tf_op jit(solution)/shard_map/ppermute | solution.py:15
  870.3 11.7 %collective-permute-start.8 = (f32[16,7168]{1,0:T(8,128)}, f32[16,7168]{1,0:T(8,128)S(1)}, u32[]{:S(2)}, u32[]{:S(2)}) collective-permute-start(f32[16,7168]{1,0:T(8,128)} %get-tuple-element.9), channel_id=1, source_target_pairs={{0,224},{32,0},{64,32},{96,64},{128,96},{160,128},{192,160},{224,1... | collective-permute-start | bytes 1376264 | tf_op jit(solution)/shard_map/ppermute | solution.py:15
  883.2 11.1 %copy-start = (f32[16,7168]{1,0:T(8,128)}, f32[16,7168]{1,0:T(8,128)S(1)}, u32[]{:S(2)}) copy-start(f32[16,7168]{1,0:T(8,128)S(1)} %sub.34) | copy-start | bytes 1376260
Sparse Core Ops, SparseCore 0:
  170.6 264.6 all-reduce.8
  600.6 268.4 all-reduce.6
where the time goes:
time: 904 us; the launch traced here: 901 us
  waiting for transfers between devices  557 us (62%)
  blocking collectives  262 us (29%)
  matrix products  26.4 us (3%)
  other arithmetic  22.5 us (2%)
  starting transfers between devices  16.7 us (2%)
  between operations  14.2 us (2%)
    psum x2, waiting for transfers between devices, body(): sum_left, sum_right = lax.psum((part_left, part_right), 'shard')  533 us
    psum x2, blocking collectives, orthonormal(): lax.psum((gram_of(raw_left), gram_of(raw_right)), 'shard')  262 us
    ppermute x9, waiting for transfers between devices, shifted(): return lax.ppermute(value, axis, pairs)  23.7 us
  transfers between devices with their start and end apart: 11, of which 7 were waited for; matrix products, arithmetic and copies ran while one was open for 0% of the time, Pallas kernels for 0%

commit v1 on v0

v1 whole, which is shorter than its diff:
```python
import functools

import jax
import jax.numpy as jnp
from jax import lax
from jax.experimental import pallas as pl
from jax.experimental.pallas import tpu as pltpu
from jax.sharding import PartitionSpec as P

STEPS = 2
RANK = 16
gossip_rate = 0.5

BF = jnp.bfloat16
F32 = jnp.float32
MESH = pl.DeviceIdType.MESH

ZS = 8
BLOCK = 896
PAD = 1024
HALF = 512
PIECE = 256
HIDDEN = 320
WIDE = 384

ORDER = (4, 3, 5, 2, 6, 1, 7, 0)
PEERS = tuple((d, e) for d in ORDER for e in (1, 0) if d or e)


def split3(x):
    hi = x.astype(BF)
    rest = x - hi.astype(F32)
    mid = rest.astype(BF)
    lo = (rest - mid.astype(F32)).astype(BF)
    return hi, mid, lo


def inverse_factors(gram):
    both = jnp.stack([gram, pltpu.roll(gram, 128 - RANK, axis=1)])
    row = lax.broadcasted_iota(jnp.int32, (2, RANK, 128), 1)
    lane = lax.broadcasted_iota(jnp.int32, (2, RANK, 128), 2)
    eye = jnp.where(lane - RANK == row, 1.0, 0.0)
    a = jnp.where(lane < RANK, both, eye)
    for k in range(RANK - 1):
        pivot = a[:, k : k + 1, :]
        m = jnp.where(row[:, :, :1] > k, a[:, :, k : k + 1] / pivot[:, :, k : k + 1], 0.0)
        a = a - m * pivot
    diagonal = jnp.sum(jnp.where(lane == row, a, 0.0), axis=2, keepdims=True)
    return a / jnp.sqrt(diagonal)


def apply_lower(inverse, x):
    total = inverse[:, RANK : RANK + 1] * x[0:1, :]
    for k in range(1, RANK):
        total = total + inverse[:, RANK + k : RANK + k + 1] * x[k : k + 1, :]
    return total


def main_kernel(
    w_hbm, f0_ref, basis_ref, fac_ref,
    w, f, xs, xr, gs, gc, gz, p, q, sb, t, dd, r, y,
    w_sem, init_s, init_r, x_s, x_r, gc_s, gc_r, gz_s, gz_r,
    q_s, q_r, t_s, t_r, r_s, r_r, az_s, az_r, ag_s, ag_r, ac_s, ac_r,
):
    g = lax.axis_index("group")
    s = lax.axis_index("shard")
    z, xh, c = s // 4, (s // 2) % 2, s % 2
    other = (g, s + 1 - 2 * c)
    left, right = ((g + 7) % 8, s), ((g + 1) % 8, s)
    across = ((g + 7 + 2 * c) % 8, s + 1 - 2 * c)
    mine = 1 - c

    def peer(d, e):
        return (g, ((z + d) % ZS) * 4 + ((xh + e) % 2) * 2 + c)

    started = []

    def send(src, dst, ss, rs, to):
        copy = pltpu.make_async_remote_copy(
            src_ref=src, dst_ref=dst, send_sem=ss, recv_sem=rs, device_id=to, device_id_type=MESH
        )
        copy.start()
        started.append(copy)
        return copy

    loads = []
    for b in range(ZS):
        load = pltpu.make_async_copy(w_hbm.at[:, pl.ds(b * BLOCK, BLOCK)], w.at[b], w_sem.at[b])
        load.start()
        loads.append(load)

    barrier = pltpu.get_barrier_semaphore()
    greeted = [other, left, right, across] + [peer(d, e) for d, e in PEERS]
    for device in greeted:
        pl.semaphore_signal(barrier, inc=1, device_id=device, device_id_type=MESH)

    for b in range(ZS):
        f[0, 1, b, :, :BLOCK] = f0_ref[:, b * BLOCK : (b + 1) * BLOCK].astype(BF)
    pl.semaphore_wait(barrier, len(greeted))

    here = pl.ds(pl.multiple_of(c * HALF, HALF), HALF)
    there = pl.ds(pl.multiple_of((1 - c) * HALF, HALF), HALF)
    first = send(f.at[0, 1, :, :, here], f.at[0, 0, :, :, here], init_s.at[0], init_r.at[0], right)
    for load in loads:
        load.wait()
    first.wait_recv()
    second = send(f.at[0, 0, :, :, here], f.at[0, 0, :, :, here], init_s.at[1], init_r.at[1], other)
    second.wait_recv()

    for step in range(STEPS):
        own = jnp.zeros((2 * RANK, HIDDEN), F32)
        for b in range(ZS):
            lhs = f[step, :, b, :, :BLOCK].reshape(2 * RANK, BLOCK)
            own = own + lax.dot_general(
                lhs, w[b], (((1,), (1,)), ((), ())), preferred_element_type=F32
            )
        own = jnp.concatenate([own, jnp.zeros((2 * RANK, WIDE - HIDDEN), F32)], axis=1)
        xs[step, 0] = own[:RANK]
        xs[step, 1] = own[RANK:]
        to_right = send(xs.at[step, 1], xr.at[step, 0], x_s.at[step, 1], x_r.at[step, 0], right)
        to_left = send(xs.at[step, 0], xr.at[step, 1], x_s.at[step, 0], x_r.at[step, 1], left)
        to_right.wait_recv()
        to_left.wait_recv()
        raw = jnp.concatenate([xr[step, 0] - own[:RANK], own[RANK:] - xr[step, 1]], axis=0)

        square = lax.dot_general(
            raw, raw, (((1,), (1,)), ((), ())),
            precision=lax.Precision.HIGHEST, preferred_element_type=F32,
        )
        square = jnp.concatenate([square, jnp.zeros((2 * RANK, 128 - 2 * RANK), F32)], axis=1)
        lane = lax.broadcasted_iota(jnp.int32, (RANK, 128), 1)
        gram = jnp.where(lane < RANK, square[:RANK], square[RANK:])
        gs[step, 0] = gram
        gram_core = send(gs.at[step, 0], gc.at[step], gc_s.at[step], gc_r.at[step], other)

        stacked = jnp.concatenate(split3(raw), axis=0)[:, :HIDDEN]
        core_copies = []
        for i, d in enumerate(ORDER):
            b = (z + d) % ZS
            prod = jnp.dot(stacked, w[b], preferred_element_type=F32)
            prod = prod[: 2 * RANK] + (prod[2 * RANK : 4 * RANK] + prod[4 * RANK :])
            p[step, 0, i, :, :BLOCK] = prod[:RANK]
            p[step, 1, i, :, :BLOCK] = prod[RANK:]
            core_copies.append(send(
                p.at[step, 1 - c, i, :, pl.ds(0, BLOCK)], q.at[step, i, :, pl.ds(0, BLOCK)],
                q_s.at[step, i], q_r.at[step, i], other,
            ))

        gram_core.wait_recv()
        gram = gram + gc[step]
        gs[step, 1] = gram
        gram_copies = [
            send(gs.at[step, 1], gz.at[step, j], gz_s.at[step, j], gz_r.at[step, j], peer(d, e))
            for j, (d, e) in enumerate(PEERS)
        ]

        cross_copies = []
        for i in range(ZS):
            core_copies[i].wait_recv()
            sb[step, i] = p[step, c, i] + q[step, i]
            cross_copies.append(send(
                sb.at[step, i, :, here], t.at[step, i], t_s.at[step, i], t_r.at[step, i], across
            ))

        sign = (2 * c - 1).astype(F32)
        reduce_copies = []
        for i, d in enumerate(ORDER):
            cross_copies[i].wait_recv()
            dd[step, i] = sign * (sb[step, i, :, there] - t[step, i])
            for e in (1, 0):
                if d or e:
                    j = len(reduce_copies)
                    part = pl.ds(pl.multiple_of(((xh + e) % 2) * PIECE, PIECE), PIECE)
                    reduce_copies.append(send(
                        dd.at[step, i, :, part], r.at[step, j],
                        r_s.at[step, j], r_r.at[step, j], peer(d, e),
                    ))

        for j, copy in enumerate(gram_copies):
            copy.wait_recv()
            gram = gram + gz[step, j]
        inverses = inverse_factors(gram)
        inverse = jnp.where(c == 0, inverses[0], inverses[1])

        own_part = pl.ds(pl.multiple_of(xh * PIECE, PIECE), PIECE)
        total = dd[step, ZS - 1, :, own_part]
        for j, copy in enumerate(reduce_copies):
            copy.wait_recv()
            total = total + r[step, j]
        piece = apply_lower(inverse, total).astype(BF)

        slot = pl.ds(pl.multiple_of(mine * HALF + xh * PIECE, PIECE), PIECE)
        y[step] = piece
        f[step + 1, c, z, :, slot] = piece
        gathers = [
            send(y.at[step], f.at[step + 1, c, z, :, slot], az_s.at[step, j], az_r.at[step, j], peer(d, e))
            for j, (d, e) in enumerate(PEERS)
        ]
        if step == STEPS - 1:
            basis_ref[:RANK] = -apply_lower(inverses[0], raw[:RANK])
            basis_ref[RANK:] = apply_lower(inverses[1], raw[RANK:])
        for copy in gathers:
            copy.wait_recv()
        half = f.at[step + 1, c, :, :, there]
        cross = send(half, f.at[step + 1, 1 - c, :, :, there], ag_s.at[step], ag_r.at[step], across)
        cross.wait_recv()
        last = send(f.at[step + 1, c], f.at[step + 1, c], ac_s.at[step], ac_r.at[step], other)
        last.wait_recv()

    fac_ref[...] = f[STEPS]
    for copy in started:
        copy.wait_send()


def update_kernel(w_ref, basis_ref, fac_ref, new_ref, next_ref, lhs):
    @pl.when(pl.program_id(0) == 0)
    def _():
        hi, mid, lo = split3(basis_ref[...] * gossip_rate)
        rows = jnp.concatenate([hi.astype(F32), mid.astype(F32), lo.astype(F32), jnp.zeros((2 * RANK, WIDE), F32)], axis=0)
        lhs[...] = rows.T.astype(BF)

    fac = fac_ref[:, 0, :, :BLOCK].reshape(2 * RANK, BLOCK)
    rhs = jnp.concatenate([fac, fac, fac, jnp.zeros_like(fac)], axis=0)
    delta = jnp.dot(lhs[:HIDDEN, :], rhs, preferred_element_type=F32)
    new_ref[0] = (w_ref[0].astype(F32) - delta).astype(BF)
    next_ref[0] = fac_ref[1, 0, :, :BLOCK].astype(F32)


def body(weights, factor_init):
    dma = pltpu.SemaphoreType.DMA
    n = len(PEERS)
    basis, fac = pl.pallas_call(
        main_kernel,
        name="rounds",
        out_shape=(
            jax.ShapeDtypeStruct((2 * RANK, WIDE), F32),
            jax.ShapeDtypeStruct((2, ZS, RANK, PAD), BF),
        ),
        in_specs=[pl.BlockSpec(memory_space=pl.ANY), pl.BlockSpec(memory_space=pltpu.VMEM)],
        out_specs=[pl.BlockSpec(memory_space=pltpu.VMEM)] * 2,
        scratch_shapes=[
            pltpu.VMEM((ZS, HIDDEN, BLOCK), BF),
            pltpu.VMEM((STEPS + 1, 2, ZS, RANK, PAD), BF),
            pltpu.VMEM((STEPS, 2, RANK, WIDE), F32),
            pltpu.VMEM((STEPS, 2, RANK, WIDE), F32),
            pltpu.VMEM((STEPS, 2, RANK, 128), F32),
            pltpu.VMEM((STEPS, RANK, 128), F32),
            pltpu.VMEM((STEPS, n, RANK, 128), F32),
            pltpu.VMEM((STEPS, 2, ZS, RANK, PAD), F32),
            pltpu.VMEM((STEPS, ZS, RANK, PAD), F32),
            pltpu.VMEM((STEPS, ZS, RANK, PAD), F32),
            pltpu.VMEM((STEPS, ZS, RANK, HALF), F32),
            pltpu.VMEM((STEPS, ZS, RANK, HALF), F32),
            pltpu.VMEM((STEPS, n, RANK, PIECE), F32),
            pltpu.VMEM((STEPS, RANK, PIECE), BF),
            dma((ZS,)),
            dma((2,)), dma((2,)),
            dma((STEPS, 2)), dma((STEPS, 2)),
            dma((STEPS,)), dma((STEPS,)),
            dma((STEPS, n)), dma((STEPS, n)),
            dma((STEPS, ZS)), dma((STEPS, ZS)),
            dma((STEPS, ZS)), dma((STEPS, ZS)),
            dma((STEPS, n)), dma((STEPS, n)),
            dma((STEPS, n)), dma((STEPS, n)),
            dma((STEPS,)), dma((STEPS,)),
            dma((STEPS,)), dma((STEPS,)),
        ],
        compiler_params=pltpu.CompilerParams(
            collective_id=0, has_side_effects=True, vmem_limit_bytes=48 * 2**20
        ),
        cost_estimate=pl.CostEstimate(
            flops=10 * 32 * HIDDEN * 7168, bytes_accessed=HIDDEN * 7168 * 2, transcendentals=0
        ),
    )(weights[0], factor_init[0])
    new, nxt = pl.pallas_call(
        update_kernel,
        name="update",
        grid=(ZS,),
        out_shape=(
            jax.ShapeDtypeStruct(weights.shape, BF),
            jax.ShapeDtypeStruct(factor_init.shape, F32),
        ),
        in_specs=[
            pl.BlockSpec((1, HIDDEN, BLOCK), lambda b: (0, 0, b)),
            pl.BlockSpec((2 * RANK, WIDE), lambda b: (0, 0)),
            pl.BlockSpec((2, 1, RANK, PAD), lambda b: (0, b, 0, 0)),
        ],
        out_specs=[
            pl.BlockSpec((1, HIDDEN, BLOCK), lambda b: (0, 0, b)),
            pl.BlockSpec((1, RANK, BLOCK), lambda b: (0, 0, b)),
        ],
        scratch_shapes=[pltpu.VMEM((WIDE, 128), BF)],
        compiler_params=pltpu.CompilerParams(vmem_limit_bytes=32 * 2**20),
        cost_estimate=pl.CostEstimate(
            flops=2 * 128 * HIDDEN * 7168, bytes_accessed=HIDDEN * 7168 * 4, transcendentals=0
        ),
    )(weights, basis, fac)
    return new, nxt


def solution(mesh):
    in_specs = (P("group", "shard", None), P("group", None, None))
    out_specs = (P("group", "shard", None), P("group", None, None))
    return jax.shard_map(body, mesh=mesh, in_specs=in_specs, out_specs=out_specs, check_vma=False)
```

time: 904 us -> 95.5 us (0.11)
  waiting for transfers between devices: 557 us -> 0 us
  blocking collectives: 262 us -> 0 us
  Pallas kernels: 0 us -> 91.4 us
  matrix products: 26.4 us -> 0 us
  other arithmetic: 22.5 us -> 0 us
  starting transfers between devices: 16.7 us -> 0 us
  between operations: 14.2 us -> 0.65 us
    psum x2 -> x0, waiting for transfers between devices: 533 us -> none  [body(): sum_left, sum_right = lax.psum((part_left, part_right), 'shard')]
    psum x2 -> x0, blocking collectives: 262 us -> none  [orthonormal(): lax.psum((gram_of(raw_left), gram_of(raw_right)), 'shard')]
    pallas_call x0 -> x2, Pallas kernels: none -> 91.4 us  [the longest x1 86.2 us: body(): pl.pallas_call(main_kernel, name='rounds', out_shape=(jax.ShapeDtypeStruc...]
    dot_general x9 -> x0, matrix products: 25.4 us -> none  [the longest x1 11.1 us: body(): lax.dot_general(signed, factors, (((0,), (0,)), ((), ())), precision=lax....]
    ppermute x9 -> x0, waiting for transfers between devices: 23.7 us -> none  [shifted(): return lax.ppermute(value, axis, pairs)]
    ppermute x9 -> x0, starting transfers between devices: 16.7 us -> none  [shifted(): return lax.ppermute(value, axis, pairs)]
    another operation x20 -> x0, other arithmetic: 16 us -> none  [the longest x12 8.54 us: solve_with(): lower = lax.linalg.cholesky(gram_matrix)]
  transfers between devices with their start and end apart: 11 -> 0, of which waited for: 7 -> 0; matrix products, arithmetic and copies ran while one was open for 0% -> 0% of each run, Pallas kernels for 0% -> 0%
where the time goes in v1:
time: 95.5 us; the launch traced here: 95.4 us
  Pallas kernels  91.4 us (96%)
  local copies, waits for them, and re-layouts  3.31 us (3%)
    pallas_call x1, Pallas kernels, body(): pl.pallas_call(main_kernel, name='rounds', out_shape=(jax.ShapeDtypeStruc...  86.2 us
    pallas_call x1, Pallas kernels, body(): pl.pallas_call(update_kernel, name='update', grid=(ZS,), out_shape=(jax.S...  5.2 us
    unnamed x4, local copies, waits for them, and re-layouts  3.31 us

profile of v1, /device:TPU:1, one launch (start us, length us, event | category | flops | bytes accessed | tf_op | source)
XLA Modules:
  0.0 95.4 jit_solution(11916818460262691398)
XLA Ops:
  0.6 0.0 copy-start
  0.6 2.3 %copy-done = bf16[1,320,7168]{2,1,0:T(8,128)(2,1)S(1)} copy-done((bf16[1,320,7168]{2,1,0:T(8,128)(2,1)S(1)}, bf16[1,320,7168]{2,1,0:T(8,128)(2,1)}, u32[]{:S(2)}) %copy-start) | copy-done | bytes 4587544
  2.9 0.0 copy-start.1
  2.9 1.0 %copy-done.1 = f32[1,16,7168]{2,1,0:T(8,128)S(1)} copy-done((f32[1,16,7168]{2,1,0:T(8,128)S(1)}, f32[1,16,7168]{2,1,0:T(8,128)}, u32[]{:S(2)}) %copy-start.1) | copy-done | bytes 458776
  3.9 86.2 %rounds.1 = (f32[32,384]{1,0:T(8,128)S(1)}, bf16[2,8,16,1024]{3,2,1,0:T(8,128)(2,1)S(1)}) custom-call(bf16[320,7168]{1,0:T(8,128)(2,1)S(1)} %bitcast.2, f32[16,7168]{1,0:T(8,128)S(1)} %bitcast.3), custom_call_target="tpu_custom_call" | custom-call | flops 734003200 | bytes 4587520 | tf_op jit(solution)/shard_map/rounds/pallas_call | solution.py:232
  90.2 5.2 %update.1 = (bf16[1,320,7168]{2,1,0:T(8,128)(2,1)}, f32[1,16,7168]{2,1,0:T(8,128)}) custom-call(bf16[1,320,7168]{2,1,0:T(8,128)(2,1)S(1)} %copy-done, f32[32,384]{1,0:T(8,128)S(1)} %get-tuple-element.4.basis_ref, bf16[2,8,16,1024]{3,2,1,0:T(8,128)(2,1)S(1)} %get-tuple-element.5.fac_ref), custom_call_target="tpu_custom_call" | custom-call | flops 587202560 | bytes 9175040 | tf_op jit(solution)/shard_map/update/pallas_call | solution.py:275
Async XLA Ops:
  0.6 2.3 %copy-start = (bf16[1,320,7168]{2,1,0:T(8,128)(2,1)S(1)}, bf16[1,320,7168]{2,1,0:T(8,128)(2,1)}, u32[]{:S(2)}) copy-start(bf16[1,320,7168]{2,1,0:T(8,128)(2,1)} %w_ref.1) | copy-start | bytes 13762564
  2.9 1.0 %copy-start.1 = (f32[1,16,7168]{2,1,0:T(8,128)S(1)}, f32[1,16,7168]{2,1,0:T(8,128)}, u32[]{:S(2)}) copy-start(f32[1,16,7168]{2,1,0:T(8,128)} %param.3) | copy-start | bytes 1376260

commit v2 on v1

v2 whole, which is shorter than its diff:
```python
import functools

import jax
import jax.numpy as jnp
from jax import lax
from jax.experimental import pallas as pl
from jax.experimental.pallas import tpu as pltpu
from jax.sharding import PartitionSpec as P

STEPS = 2
RANK = 16
gossip_rate = 0.5

BF = jnp.bfloat16
F32 = jnp.float32
MESH = pl.DeviceIdType.MESH

ZS = 8
BLOCK = 896
SKEW = 384
PART = 512
TILE = 128
HIDDEN = 320
BOTH = 640

ORDER = (4, 3, 5, 2, 6, 1, 7, 0)
GRAM_AT = 1
PEERS = tuple((d, e) for d in ORDER for e in (1, 0) if d or e)


def split3(x):
    hi = x.astype(BF)
    rest = x - hi.astype(F32)
    mid = rest.astype(BF)
    lo = (rest - mid.astype(F32)).astype(BF)
    return hi, mid, lo


def inverse_factors(gram):
    both = jnp.stack([gram, pltpu.roll(gram, 128 - RANK, axis=1)])
    row = lax.broadcasted_iota(jnp.int32, (2, RANK, 128), 1)
    lane = lax.broadcasted_iota(jnp.int32, (2, RANK, 128), 2)
    eye = jnp.where(lane - RANK == row, 1.0, 0.0)
    a = jnp.where(lane < RANK, both, eye)
    for k in range(RANK - 1):
        pivot = a[:, k : k + 1, :]
        m = jnp.where(row[:, :, :1] > k, a[:, :, k : k + 1] / pivot[:, :, k : k + 1], 0.0)
        a = a - m * pivot
    diagonal = jnp.sum(jnp.where(lane == row, a, 0.0), axis=2, keepdims=True)
    return a / jnp.sqrt(diagonal)


def apply_lower(inverse, x):
    total = inverse[:, RANK : RANK + 1] * x[0:1, :]
    for k in range(1, RANK):
        total = total + inverse[:, RANK + k : RANK + k + 1] * x[k : k + 1, :]
    return total


def main_kernel(
    w_hbm, f0_hbm, lhs_ref, fac_ref,
    w, f0, f, xs, xc, xo, xr, gs, gz, pk, ps, pr, dd, r, fo, bt,
    w_sem, f0_sem, wx_s, wx_r, init_s, init_r, c_s, c_r, x_s, x_r, gz_s, gz_r,
    p_s, p_r, r_s, r_r, az_s, az_r, ag_s, ag_r, ac_s, ac_r,
):
    g = lax.axis_index("group")
    s = lax.axis_index("shard")
    z, xh, c = s // 4, (s // 2) % 2, s % 2
    other = (g, s + 1 - 2 * c)
    left, right = ((g + 7) % 8, s), ((g + 1) % 8, s)

    def peer(d, e):
        return (g, ((z + d) % ZS) * 4 + ((xh + e) % 2) * 2 + c)

    started = []

    def send(src, dst, ss, rs, to):
        copy = pltpu.make_async_remote_copy(
            src_ref=src, dst_ref=dst, send_sem=ss, recv_sem=rs, device_id=to, device_id_type=MESH
        )
        copy.start()
        started.append(copy)
        return copy

    def columns(b, core):
        return pl.ds(pl.multiple_of(b * BLOCK + core * SKEW, TILE), PART)

    f0_load = pltpu.make_async_copy(f0_hbm, f0, f0_sem)
    f0_load.start()
    loads = []
    for b in range(ZS):
        load = pltpu.make_async_copy(w_hbm.at[:, columns(b, c)], w.at[b, c], w_sem.at[b])
        load.start()
        loads.append(load)

    barrier = pltpu.get_barrier_semaphore()
    greeted = [other, left, right] + [peer(d, e) for d, e in PEERS]
    for device in greeted:
        pl.semaphore_signal(barrier, inc=1, device_id=device, device_id_type=MESH)

    f0_load.wait()
    for b in range(ZS):
        for t in range(4):
            tile = pl.ds(pl.multiple_of(b * BLOCK + c * SKEW + t * TILE, TILE), TILE)
            f[0, t // 2, b, t % 2, 1] = f0[:, tile].astype(BF)
    pl.semaphore_wait(barrier, len(greeted))

    arrive = [
        send(f.at[0, kind, :, :, 1], f.at[0, 1 - kind, :, :, 0], init_s.at[kind], init_r.at[kind], right)
        for kind in range(2)
    ]
    for b in range(ZS):
        arrive.append(send(w_hbm.at[:, columns(b, 1 - c)], w.at[b, c], wx_s.at[b], wx_r.at[b], other))
    for load in loads:
        load.wait()
    for copy in arrive:
        copy.wait_recv()

    for step in range(STEPS):
        part = jnp.zeros((2 * RANK, BOTH), F32)
        for b in range(ZS):
            tiles = []
            for t in range(4):
                k = t // 2
                tile = jnp.concatenate([f[step, 1 - k, b, t % 2, 0], f[step, k, b, t % 2, 1]], axis=0)
                if t == 0:
                    tile = jnp.where(c == 1, jnp.zeros_like(tile), tile)
                tiles.append(tile)
            part = part + lax.dot_general(
                jnp.concatenate(tiles, axis=1), w[b].reshape(BOTH, PART),
                (((1,), (1,)), ((), ())), preferred_element_type=F32,
            )
        xs[step, 0] = part[:RANK]
        xs[step, 1] = part[RANK:]
        core_copy = send(xs.at[step], xc.at[step], c_s.at[step], c_r.at[step], other)
        core_copy.wait_recv()
        own_left = part[:RANK] + xc[step, 0]
        own_right = part[RANK:] + xc[step, 1]
        xo[step, 0] = own_left
        xo[step, 1] = own_right
        to_right = send(xo.at[step, 1], xr.at[step, 0], x_s.at[step, 1], x_r.at[step, 0], right)
        to_left = send(xo.at[step, 0], xr.at[step, 1], x_s.at[step, 0], x_r.at[step, 1], left)
        to_right.wait_recv()
        to_left.wait_recv()
        raw = jnp.concatenate([xr[step, 0] - own_left, own_right - xr[step, 1]], axis=0)

        stacked = jnp.concatenate(split3(raw), axis=0)
        cross_copies = []
        for i, d in enumerate(ORDER):
            b = (z + d) % ZS
            prod = jnp.dot(stacked, w[b].reshape(BOTH, PART), preferred_element_type=F32)
            prod = prod[: 2 * RANK] + (prod[2 * RANK : 4 * RANK] + prod[4 * RANK :])
            half = PART // 2
            ps[step, i, 0] = prod[:RANK, :half]
            ps[step, i, 1] = prod[RANK:, half:]
            pk[step, i, 0] = prod[:RANK, half:]
            pk[step, i, 1] = prod[RANK:, :half]
            cross_copies.append((
                send(ps.at[step, i, 1], pr.at[step, i, 0], p_s.at[step, i, 1], p_r.at[step, i, 0], right),
                send(ps.at[step, i, 0], pr.at[step, i, 1], p_s.at[step, i, 0], p_r.at[step, i, 1], left),
            ))
            if i == GRAM_AT:
                square = lax.dot_general(
                    raw, raw, (((1,), (1,)), ((), ())),
                    precision=lax.Precision.HIGHEST, preferred_element_type=F32,
                )
                square = jnp.concatenate([square, jnp.zeros((2 * RANK, TILE - 2 * RANK), F32)], axis=1)
                lane = lax.broadcasted_iota(jnp.int32, (RANK, TILE), 1)
                gram = jnp.where(lane < RANK, square[:RANK], square[RANK:])
                gs[step] = gram
                gram_copies = [
                    send(gs.at[step], gz.at[step, j], gz_s.at[step, j], gz_r.at[step, j], peer(d2, e2))
                    for j, (d2, e2) in enumerate(PEERS)
                ]

        reduce_copies = []
        for i, d in enumerate(ORDER):
            for copy in cross_copies[i]:
                copy.wait_recv()
            diff_left = pr[step, i, 0] - pk[step, i, 0]
            diff_right = pk[step, i, 1] - pr[step, i, 1]
            for t in range(2):
                dd[step, i, t, 0] = diff_left[:, t * TILE : (t + 1) * TILE]
                dd[step, i, t, 1] = diff_right[:, t * TILE : (t + 1) * TILE]
            for e in (1, 0):
                if d or e:
                    j = len(reduce_copies)
                    reduce_copies.append(send(
                        dd.at[step, i, (xh + e) % 2], r.at[step, j],
                        r_s.at[step, j], r_r.at[step, j], peer(d, e),
                    ))

        for j, copy in enumerate(gram_copies):
            copy.wait_recv()
            gram = gram + gz[step, j]
        inverses = inverse_factors(gram)

        total = dd[step, ZS - 1, xh]
        for j, copy in enumerate(reduce_copies):
            copy.wait_recv()
            total = total + r[step, j]

        f[step + 1, 0, z, xh, 0] = apply_lower(inverses[0], total[0]).astype(BF)
        f[step + 1, 0, z, xh, 1] = apply_lower(inverses[1], total[1]).astype(BF)
        piece = f.at[step + 1, 0, z, xh]
        gathers = [
            send(piece, piece, az_s.at[step, j], az_r.at[step, j], peer(d, e))
            for j, (d, e) in enumerate(PEERS)
        ]
        if step == STEPS - 1:
            basis = gossip_rate * jnp.concatenate(
                [-apply_lower(inverses[0], raw[:RANK]), apply_lower(inverses[1], raw[RANK:])], axis=0
            )
            terms = [term.astype(F32) for term in split3(basis)]
            bt[...] = jnp.concatenate(terms + [jnp.zeros((2 * RANK, BOTH), F32)], axis=0).T
            lhs_ref[...] = bt[pl.ds(pl.multiple_of(c * HIDDEN, 16), HIDDEN), :].astype(BF)
        for copy in gathers:
            copy.wait_recv()
        to_right = send(
            f.at[step + 1, 0, :, :, 1], f.at[step + 1, 1, :, :, 0], ag_s.at[step, 1], ag_r.at[step, 0], right
        )
        to_left = send(
            f.at[step + 1, 0, :, :, 0], f.at[step + 1, 1, :, :, 1], ag_s.at[step, 0], ag_r.at[step, 1], left
        )
        to_right.wait_recv()
        to_left.wait_recv()

    last = send(f.at[STEPS], fo, ac_s, ac_r, other)
    fac_ref[c] = f[STEPS]
    last.wait_recv()
    fac_ref[1 - c] = fo[...]
    for copy in started:
        copy.wait_send()


def update_kernel(w_ref, lhs_ref, fac_ref, new_ref, next_ref):
    tiles = []
    for core in range(2):
        for t in range(core, 4):
            k = t // 2
            tiles.append(jnp.concatenate(
                [fac_ref[core, 1 - k, 0, t % 2, 0], fac_ref[core, k, 0, t % 2, 1]], axis=0
            ))
    fac = jnp.concatenate(tiles, axis=1)
    rhs = jnp.concatenate([fac, fac, fac, jnp.zeros_like(fac)], axis=0)
    delta = jnp.dot(lhs_ref[...], rhs, preferred_element_type=F32)
    new_ref[0] = (w_ref[0].astype(F32) - delta).astype(BF)
    next_ref[0] = fac[RANK:].astype(F32)


def body(weights, factor_init):
    dma = pltpu.SemaphoreType.DMA
    n = len(PEERS)
    lhs, fac = pl.pallas_call(
        main_kernel,
        name="rounds",
        out_shape=(
            jax.ShapeDtypeStruct((HIDDEN, TILE), BF),
            jax.ShapeDtypeStruct((2, 2, ZS, 2, 2, RANK, TILE), BF),
        ),
        in_specs=[pl.BlockSpec(memory_space=pl.ANY)] * 2,
        out_specs=[pl.BlockSpec(memory_space=pltpu.VMEM)] * 2,
        scratch_shapes=[
            pltpu.VMEM((ZS, 2, HIDDEN, PART), BF),
            pltpu.VMEM((RANK, ZS * BLOCK), F32),
            pltpu.VMEM((STEPS + 1, 2, ZS, 2, 2, RANK, TILE), BF),
            pltpu.VMEM((STEPS, 2, RANK, BOTH), F32),
            pltpu.VMEM((STEPS, 2, RANK, BOTH), F32),
            pltpu.VMEM((STEPS, 2, RANK, BOTH), F32),
            pltpu.VMEM((STEPS, 2, RANK, BOTH), F32),
            pltpu.VMEM((STEPS, RANK, TILE), F32),
            pltpu.VMEM((STEPS, n, RANK, TILE), F32),
            pltpu.VMEM((STEPS, ZS, 2, RANK, PART // 2), F32),
            pltpu.VMEM((STEPS, ZS, 2, RANK, PART // 2), F32),
            pltpu.VMEM((STEPS, ZS, 2, RANK, PART // 2), F32),
            pltpu.VMEM((STEPS, ZS, 2, 2, RANK, TILE), F32),
            pltpu.VMEM((STEPS, n, 2, RANK, TILE), F32),
            pltpu.VMEM((2, ZS, 2, 2, RANK, TILE), BF),
            pltpu.VMEM((BOTH, TILE), F32),
            dma((ZS,)), dma(()),
            dma((ZS,)), dma((ZS,)),
            dma((2,)), dma((2,)),
            dma((STEPS,)), dma((STEPS,)),
            dma((STEPS, 2)), dma((STEPS, 2)),
            dma((STEPS, n)), dma((STEPS, n)),
            dma((STEPS, ZS, 2)), dma((STEPS, ZS, 2)),
            dma((STEPS, n)), dma((STEPS, n)),
            dma((STEPS, n)), dma((STEPS, n)),
            dma((STEPS, 2)), dma((STEPS, 2)),
            dma(()), dma(()),
        ],
        compiler_params=pltpu.CompilerParams(
            collective_id=0, has_side_effects=True, vmem_limit_bytes=60 * 2**20
        ),
        cost_estimate=pl.CostEstimate(
            flops=10 * 32 * HIDDEN * 7168, bytes_accessed=HIDDEN * 7168 * 2, transcendentals=0
        ),
    )(weights[0], factor_init[0])
    new, nxt = pl.pallas_call(
        update_kernel,
        name="update",
        grid=(ZS,),
        out_shape=(
            jax.ShapeDtypeStruct(weights.shape, BF),
            jax.ShapeDtypeStruct(factor_init.shape, F32),
        ),
        in_specs=[
            pl.BlockSpec((1, HIDDEN, BLOCK), lambda b: (0, 0, b)),
            pl.BlockSpec((HIDDEN, TILE), lambda b: (0, 0)),
            pl.BlockSpec((2, 2, 1, 2, 2, RANK, TILE), lambda b: (0, 0, b, 0, 0, 0, 0)),
        ],
        out_specs=[
            pl.BlockSpec((1, HIDDEN, BLOCK), lambda b: (0, 0, b)),
            pl.BlockSpec((1, RANK, BLOCK), lambda b: (0, 0, b)),
        ],
        compiler_params=pltpu.CompilerParams(vmem_limit_bytes=32 * 2**20),
        cost_estimate=pl.CostEstimate(
            flops=2 * 128 * HIDDEN * 7168, bytes_accessed=HIDDEN * 7168 * 4, transcendentals=0
        ),
    )(weights, lhs, fac)
    return new, nxt


def solution(mesh):
    in_specs = (P("group", "shard", None), P("group", None, None))
    out_specs = (P("group", "shard", None), P("group", None, None))
    return jax.shard_map(body, mesh=mesh, in_specs=in_specs, out_specs=out_specs, check_vma=False)
```

time: 95.5 us -> 92.2 us (0.965)
  Pallas kernels: 91.4 us -> 87.1 us
    pallas_call x1, Pallas kernels: 86.2 us -> 82 us  [body(): pl.pallas_call(main_kernel, name='rounds', out_shape=(jax.ShapeDtypeStruc...]
    unnamed x4 -> x6, local copies, waits for them, and re-layouts: 3.31 us -> 4.22 us
where the time goes in v2:
time: 92.2 us; the launch traced here: 92 us
  Pallas kernels  87.1 us (94%)
  local copies, waits for them, and re-layouts  4.22 us (5%)
    pallas_call x1, Pallas kernels, body(): pl.pallas_call(main_kernel, name='rounds', out_shape=(jax.ShapeDtypeStruc...  82 us
    pallas_call x1, Pallas kernels, body(): pl.pallas_call(update_kernel, name='update', grid=(ZS,), out_shape=(jax.S...  5.05 us
    unnamed x6, local copies, waits for them, and re-layouts  4.22 us

profile of v2, /device:TPU:1, one launch (start us, length us, event | category | flops | bytes accessed | tf_op | source)
XLA Modules:
  0.0 92.0 jit_solution(8185864189959295761)
XLA Ops:
  0.6 82.0 %rounds.1 = (bf16[320,128]{1,0:T(8,128)(2,1)}, bf16[2,2,8,2,2,16,128]{6,5,4,3,2,1,0:T(8,128)(2,1)}) custom-call(bf16[320,7168]{1,0:T(8,128)(2,1)} %bitcast.2, f32[16,7168]{1,0:T(8,128)} %bitcast.3), custom_call_target="tpu_custom_call" | custom-call | flops 734003200 | bytes 4587520 | tf_op jit(solution)/shard_map/rounds/pallas_call | solution.py:254
  82.7 0.0 copy-start
  82.7 2.3 %copy-done = bf16[1,320,7168]{2,1,0:T(8,128)(2,1)S(1)} copy-done((bf16[1,320,7168]{2,1,0:T(8,128)(2,1)S(1)}, bf16[1,320,7168]{2,1,0:T(8,128)(2,1)}, u32[]{:S(2)}) %copy-start) | copy-done | bytes 4587544
  85.0 0.0 copy-start.1
  85.0 1.0 %copy-done.1 = bf16[2,2,8,2,2,16,128]{6,5,4,3,2,1,0:T(8,128)(2,1)S(1)} copy-done((bf16[2,2,8,2,2,16,128]{6,5,4,3,2,1,0:T(8,128)(2,1)S(1)}, bf16[2,2,8,2,2,16,128]{6,5,4,3,2,1,0:T(8,128)(2,1)}, u32[]{:S(2)}) %copy-start.1) | copy-done | bytes 524312
  86.0 0.0 copy-start.2
  86.0 0.9 copy-done.2
  86.9 5.0 %update.1 = (bf16[1,320,7168]{2,1,0:T(8,128)(2,1)}, f32[1,16,7168]{2,1,0:T(8,128)}) custom-call(bf16[1,320,7168]{2,1,0:T(8,128)(2,1)S(1)} %copy-done, bf16[320,128]{1,0:T(8,128)(2,1)S(1)} %copy-done.2, bf16[2,2,8,2,2,16,128]{6,5,4,3,2,1,0:T(8,128)(2,1)S(1)} %copy-done.1), custom_call_target="tpu_custom_call" | custom-call | flops 587202560 | bytes 9175040 | tf_op jit(solution)/shard_map/update/pallas_call | solution.py:299
Async XLA Ops:
  82.7 2.3 %copy-start = (bf16[1,320,7168]{2,1,0:T(8,128)(2,1)S(1)}, bf16[1,320,7168]{2,1,0:T(8,128)(2,1)}, u32[]{:S(2)}) copy-start(bf16[1,320,7168]{2,1,0:T(8,128)(2,1)} %w_ref.1) | copy-start | bytes 13762564
  85.0 1.0 %copy-start.1 = (bf16[2,2,8,2,2,16,128]{6,5,4,3,2,1,0:T(8,128)(2,1)S(1)}, bf16[2,2,8,2,2,16,128]{6,5,4,3,2,1,0:T(8,128)(2,1)}, u32[]{:S(2)}) copy-start(bf16[2,2,8,2,2,16,128]{6,5,4,3,2,1,0:T(8,128)(2,1)} %get-tuple-element.5.fac_ref) | copy-start | bytes 1572868
  86.0 0.9 copy-start.2

commit v3 on v2

v3 whole, which is shorter than its diff:
```python
import functools

import jax
import jax.numpy as jnp
from jax import lax
from jax.experimental import pallas as pl
from jax.experimental.pallas import tpu as pltpu
from jax.sharding import PartitionSpec as P

STEPS = 2
RANK = 16
gossip_rate = 0.5

BF = jnp.bfloat16
F32 = jnp.float32
MESH = pl.DeviceIdType.MESH

ZS = 8
BLOCK = 896
SKEW = 384
PART = 512
TILE = 128
HIDDEN = 320
BOTH = 640

ORDER = (4, 3, 5, 2, 6, 1, 7, 0)
NEAR = (0, 1, 7, 2, 6, 3, 5, 4)
GRAM_AT = 1
GRAM_ON = 2
ALL = tuple((d, e) for d in ORDER for e in (1, 0))
PEERS = tuple((d, e) for d in ORDER for e in (1, 0) if d or e)


def split3(x):
    hi = x.astype(BF)
    rest = x - hi.astype(F32)
    mid = rest.astype(BF)
    lo = (rest - mid.astype(F32)).astype(BF)
    return hi, mid, lo


def pack_gram(square):
    wide = jnp.concatenate([square, jnp.zeros((2 * RANK, TILE - 2 * RANK), F32)], axis=1)
    lane = lax.broadcasted_iota(jnp.int32, (8, TILE), 1)
    packed = jnp.where(lane < RANK, wide[:8], pltpu.roll(wide[8:16], RANK, axis=1))
    packed = jnp.where(lane < 2 * RANK, packed, pltpu.roll(wide[16:24], RANK, axis=1))
    return jnp.where(lane < 3 * RANK, packed, pltpu.roll(wide[24:], 2 * RANK, axis=1))


def inverse_factors(packed):
    rolled = [packed] + [pltpu.roll(packed, TILE - k * RANK, axis=1) for k in range(1, 4)]
    both = jnp.concatenate(rolled, axis=0).reshape(2, RANK, TILE)
    row = lax.broadcasted_iota(jnp.int32, (2, RANK, TILE), 1)
    lane = lax.broadcasted_iota(jnp.int32, (2, RANK, TILE), 2)
    eye = jnp.where(lane - RANK == row, 1.0, 0.0)
    a = jnp.where(lane < RANK, both, eye)
    for k in range(RANK - 1):
        pivot = a[:, k : k + 1, :]
        m = jnp.where(row[:, :, :1] > k, a[:, :, k : k + 1] / pivot[:, :, k : k + 1], 0.0)
        a = a - m * pivot
    diagonal = jnp.sum(jnp.where(lane == row, a, 0.0), axis=2, keepdims=True)
    return a / jnp.sqrt(diagonal)


def apply_lower(inverse, x):
    total = inverse[:, RANK : RANK + 1] * x[0:1, :]
    for k in range(1, RANK):
        total = total + inverse[:, RANK + k : RANK + k + 1] * x[k : k + 1, :]
    return total


def main_kernel(
    w_hbm, f0, lhs_ref, fac_ref,
    w, f, xs, xc, xr, gs, gx, gz, pk, ps, pr, dd, r, bt,
    hop, w_sem, wx_s, wx_r, init_s, init_r, c_s, c_r, x_s, x_r, gx_s, gx_r, gz_s, gz_r,
    p_s, p_r, r_s, r_r, az_s, az_r, ag_s, ag_r, ac_s, ac_r,
):
    g = lax.axis_index("group")
    s = lax.axis_index("shard")
    z, xh, c = s // 4, (s // 2) % 2, s % 2
    other = (g, s + 1 - 2 * c)
    left, right = ((g + 7) % 8, s), ((g + 1) % 8, s)

    def peer(d, e):
        return (g, ((z + d) % ZS) * 4 + ((xh + e) % 2) * 2 + c)

    started = []

    def send(src, dst, ss, rs, to):
        copy = pltpu.make_async_remote_copy(
            src_ref=src, dst_ref=dst, send_sem=ss, recv_sem=rs, device_id=to, device_id_type=MESH
        )
        copy.start()
        started.append(copy)
        return copy

    def columns(b, core):
        return pl.ds(pl.multiple_of(b * BLOCK + core * SKEW, TILE), PART)

    beyond = [((g + k) % 8, s + 1 - 2 * c) for k in (7, 1)]
    barrier = pltpu.get_barrier_semaphore()
    above, below = peer(1, 0), peer(7, 0)
    aside = [((g + k) % 8, peer(0, 1)[1]) for k in (7, 1)]
    greeted = [other, left, right, above, below, peer(0, 1)] + beyond + aside
    for device in greeted:
        pl.semaphore_signal(barrier, inc=1, device_id=device, device_id_type=MESH)

    loads = []
    for b in range(ZS):
        load = pltpu.make_async_copy(w_hbm.at[:, columns(b, c)], w.at[b, c], w_sem.at[b])
        load.start()
        loads.append(load)

    for b in range(ZS):
        for t in range(4):
            tile = pl.ds(pl.multiple_of(b * BLOCK + c * SKEW + t * TILE, TILE), TILE)
            f[0, b, t // 2, t % 2, 1] = f0[:, tile].astype(BF)
    pl.semaphore_wait(barrier, len(greeted))

    first, swaps = [], []
    for b in range(ZS):
        if b % 2 == 0:
            two = pl.ds(b, 2)
            first.append([
                send(
                    f.at[0, two, k, :, 1], f.at[0, two, 1 - k, :, 0],
                    init_s.at[b // 2, k], init_r.at[b // 2, 1 - k], right,
                )
                for k in range(2)
            ])
        swaps.append(send(w_hbm.at[:, columns(b, 1 - c)], w.at[b, c], wx_s.at[b], wx_r.at[b], other))

    def tell(k):
        for way, device in enumerate((above, below)):
            pl.semaphore_signal(hop.at[k, way], inc=1, device_id=device, device_id_type=MESH)

    def hear(k):
        for way in range(2):
            pl.semaphore_wait(hop.at[k, way], 1)

    tell(0)
    gathers = {}
    for step in range(STEPS):
        part = jnp.zeros((2 * RANK, BOTH), F32)
        for i, d in enumerate(NEAR):
            if step == 0:
                b = i
                if i == 4:
                    hear(0)
                    tell(1)
                loads[b].wait()
                swaps[b].wait_recv()
                if b % 2 == 0:
                    for copy in first[b // 2]:
                        copy.wait_recv()
            else:
                b = (z + ZS - d) % ZS
                for e in range(2):
                    for copy in gathers[d, e]:
                        copy.wait_recv()
            tiles = []
            for t in range(4):
                k = t // 2
                tile = jnp.concatenate([f[step, b, 1 - k, t % 2, 0], f[step, b, k, t % 2, 1]], axis=0)
                if t == 0:
                    tile = jnp.where(c == 1, jnp.zeros_like(tile), tile)
                tiles.append(tile)
            part = part + lax.dot_general(
                jnp.concatenate(tiles, axis=1), w[b].reshape(BOTH, PART),
                (((1,), (1,)), ((), ())), preferred_element_type=F32,
            )
        xs[step, 0] = part[:RANK]
        xs[step, 1] = part[RANK:]
        if step == 0:
            hear(1)
            tell(2)
        swapped = [
            send(xs.at[step, side], xr.at[step, far, 1 - side], x_s.at[step, far, side], x_r.at[step, far, 1 - side], to)
            for side, same in ((1, right), (0, left))
            for far, to in ((0, same), (1, beyond[side]))
        ]
        swapped.append(send(xs.at[step], xc.at[step], c_s.at[step], c_r.at[step], other))
        for copy in swapped:
            copy.wait_recv()
        raw = jnp.concatenate([
            (xr[step, 0, 0] + xr[step, 1, 0]) - (part[:RANK] + xc[step, 0]),
            (part[RANK:] + xc[step, 1]) - (xr[step, 0, 1] + xr[step, 1, 1]),
        ], axis=0)

        if step == 0:
            hear(2)
            tell(3)

        stacked = jnp.concatenate(split3(raw), axis=0)
        cross_copies = []
        for i, d in enumerate(ORDER):
            b = (z + d) % ZS
            prod = jnp.dot(stacked, w[b].reshape(BOTH, PART), preferred_element_type=F32)
            prod = prod[: 2 * RANK] + (prod[2 * RANK : 4 * RANK] + prod[4 * RANK :])
            half = PART // 2
            ps[step, i, 0] = prod[:RANK, :half]
            ps[step, i, 1] = prod[RANK:, half:]
            pk[step, i, 0] = prod[:RANK, half:]
            pk[step, i, 1] = prod[RANK:, :half]
            cross_copies.append((
                send(ps.at[step, i, 1], pr.at[step, i, 0], p_s.at[step, i, 1], p_r.at[step, i, 0], right),
                send(ps.at[step, i, 0], pr.at[step, i, 1], p_s.at[step, i, 0], p_r.at[step, i, 1], left),
            ))
            if i == GRAM_AT:
                square = lax.dot_general(
                    raw, raw, (((1,), (1,)), ((), ())),
                    precision=lax.Precision.HIGHEST, preferred_element_type=F32,
                )
                gram = pack_gram(square)
                gs[step, 0] = gram
                gram_x = send(gs.at[step, 0], gx.at[step], gx_s.at[step], gx_r.at[step], peer(0, 1))

        reduce_copies = []
        for i, d in enumerate(ORDER):
            if i == 0 and step == 0:
                hear(3)
            if i == GRAM_ON:
                gram_x.wait_recv()
                gram = gram + gx[step]
                gs[step, 1] = gram
                gram_copies = [
                    send(gs.at[step, 1], gz.at[step, j], gz_s.at[step, j], gz_r.at[step, j], peer(d2, 0))
                    for j, d2 in enumerate(ORDER[:-1])
                ]
            for copy in cross_copies[i]:
                copy.wait_recv()
            diff_left = pr[step, i, 0] - pk[step, i, 0]
            diff_right = pk[step, i, 1] - pr[step, i, 1]
            for t in range(2):
                dd[step, i, t, 0] = diff_left[:, t * TILE : (t + 1) * TILE]
                dd[step, i, t, 1] = diff_right[:, t * TILE : (t + 1) * TILE]
            for e in (1, 0):
                if d or e:
                    j = len(reduce_copies)
                    reduce_copies.append(send(
                        dd.at[step, i, (xh + e) % 2], r.at[step, j],
                        r_s.at[step, j], r_r.at[step, j], peer(d, e),
                    ))

        for j, copy in enumerate(gram_copies):
            copy.wait_recv()
            gram = gram + gz[step, j]
        inverses = inverse_factors(gram)

        total = dd[step, ZS - 1, xh]
        for j, copy in enumerate(reduce_copies):
            copy.wait_recv()
            total = total + r[step, j]

        f[step + 1, z, 0, xh, 0] = apply_lower(inverses[0], total[0]).astype(BF)
        f[step + 1, z, 0, xh, 1] = apply_lower(inverses[1], total[1]).astype(BF)
        piece = f.at[step + 1, z, 0, xh]
        gathers = {}
        for j, (d, e) in enumerate(ALL):
            shard = peer(d, e)[1]
            gathers[d, e] = [
                send(
                    piece.at[side], f.at[step + 1, z, 1, xh, 1 - side],
                    ag_s.at[step, j, side], ag_r.at[step, j, 1 - side], (group, shard),
                )
                for side, group in ((1, (g + 1) % 8), (0, (g + 7) % 8))
            ]
            if d or e:
                gathers[d, e].append(send(piece, piece, az_s.at[step, j], az_r.at[step, j], (g, shard)))
        if step == STEPS - 1:
            basis = gossip_rate * jnp.concatenate(
                [-apply_lower(inverses[0], raw[:RANK]), apply_lower(inverses[1], raw[RANK:])], axis=0
            )
            terms = [term.astype(F32) for term in split3(basis)]
            bt[...] = jnp.concatenate(terms + [jnp.zeros((2 * RANK, BOTH), F32)], axis=0).T
            lhs_ref[...] = bt[pl.ds(pl.multiple_of(c * HIDDEN, 16), HIDDEN), :].astype(BF)

    lasts = []
    for i, d in enumerate(NEAR):
        b = (z + ZS - d) % ZS
        for e in range(2):
            for copy in gathers[d, e]:
                copy.wait_recv()
        lasts.append(send(f.at[STEPS, b], fac_ref.at[c, b], ac_s.at[i], ac_r.at[i], other))
        fac_ref[c, b] = f[STEPS, b]
    for copy in lasts:
        copy.wait_recv()
    for copy in started:
        copy.wait_send()


def update_kernel(w_ref, lhs_ref, fac_ref, new_hbm, next_hbm, new, nxt, new_sem, next_sem):
    stores = []
    for b in range(ZS):
        tiles = []
        for core in range(2):
            for t in range(core, 4):
                k = t // 2
                tiles.append(jnp.concatenate(
                    [fac_ref[core, b, 1 - k, t % 2, 0], fac_ref[core, b, k, t % 2, 1]], axis=0
                ))
        fac = jnp.concatenate(tiles, axis=1)
        rhs = jnp.concatenate([fac, fac, fac, jnp.zeros_like(fac)], axis=0)
        delta = jnp.dot(lhs_ref[...], rhs, preferred_element_type=F32)
        columns = slice(b * BLOCK, (b + 1) * BLOCK)
        new[b] = (w_ref[0, :, columns].astype(F32) - delta).astype(BF)
        store = pltpu.make_async_copy(new.at[b], new_hbm.at[0, :, columns], new_sem.at[b])
        store.start()
        stores.append(store)
        nxt[:, columns] = fac[RANK:].astype(F32)
    store = pltpu.make_async_copy(nxt, next_hbm.at[0], next_sem)
    store.start()
    for copy in [*stores, store]:
        copy.wait()


def body(weights, factor_init):
    dma = pltpu.SemaphoreType.DMA
    n = len(PEERS)
    lhs, fac = pl.pallas_call(
        main_kernel,
        name="rounds",
        out_shape=(
            jax.ShapeDtypeStruct((HIDDEN, TILE), BF),
            jax.ShapeDtypeStruct((2, ZS, 2, 2, 2, RANK, TILE), BF),
        ),
        in_specs=[pl.BlockSpec(memory_space=pltpu.HBM), pl.BlockSpec(memory_space=pltpu.VMEM)],
        out_specs=[pl.BlockSpec(memory_space=pltpu.VMEM)] * 2,
        scratch_shapes=[
            pltpu.VMEM((ZS, 2, HIDDEN, PART), BF),
            pltpu.VMEM((STEPS + 1, ZS, 2, 2, 2, RANK, TILE), BF),
            pltpu.VMEM((STEPS, 2, RANK, BOTH), F32),
            pltpu.VMEM((STEPS, 2, RANK, BOTH), F32),
            pltpu.VMEM((STEPS, 2, 2, RANK, BOTH), F32),
            pltpu.VMEM((STEPS, 2, 8, TILE), F32),
            pltpu.VMEM((STEPS, 8, TILE), F32),
            pltpu.VMEM((STEPS, ZS - 1, 8, TILE), F32),
            pltpu.VMEM((STEPS, ZS, 2, RANK, PART // 2), F32),
            pltpu.VMEM((STEPS, ZS, 2, RANK, PART // 2), F32),
            pltpu.VMEM((STEPS, ZS, 2, RANK, PART // 2), F32),
            pltpu.VMEM((STEPS, ZS, 2, 2, RANK, TILE), F32),
            pltpu.VMEM((STEPS, n, 2, RANK, TILE), F32),
            pltpu.VMEM((BOTH, TILE), F32),
            pltpu.SemaphoreType.REGULAR((4, 2)),
            dma((ZS,)),
            dma((ZS,)), dma((ZS,)),
            dma((ZS // 2, 2)), dma((ZS // 2, 2)),
            dma((STEPS,)), dma((STEPS,)),
            dma((STEPS, 2, 2)), dma((STEPS, 2, 2)),
            dma((STEPS,)), dma((STEPS,)),
            dma((STEPS, ZS - 1)), dma((STEPS, ZS - 1)),
            dma((STEPS, ZS, 2)), dma((STEPS, ZS, 2)),
            dma((STEPS, n)), dma((STEPS, n)),
            dma((STEPS, n + 1)), dma((STEPS, n + 1)),
            dma((STEPS, n + 1, 2)), dma((STEPS, n + 1, 2)),
            dma((ZS,)), dma((ZS,)),
        ],
        compiler_params=pltpu.CompilerParams(
            collective_id=0, has_side_effects=True, vmem_limit_bytes=52 * 2**20
        ),
        cost_estimate=pl.CostEstimate(
            flops=10 * 32 * HIDDEN * 7168, bytes_accessed=HIDDEN * 7168 * 2, transcendentals=0
        ),
    )(weights[0], factor_init[0])
    new, nxt = pl.pallas_call(
        update_kernel,
        name="update",
        out_shape=(
            jax.ShapeDtypeStruct(weights.shape, BF),
            jax.ShapeDtypeStruct(factor_init.shape, F32),
        ),
        in_specs=[pl.BlockSpec(memory_space=pltpu.VMEM)] * 3,
        out_specs=[pl.BlockSpec(memory_space=pl.ANY)] * 2,
        scratch_shapes=[
            pltpu.VMEM((ZS, HIDDEN, BLOCK), BF),
            pltpu.VMEM((RANK, ZS * BLOCK), F32),
            pltpu.SemaphoreType.DMA((ZS,)),
            pltpu.SemaphoreType.DMA(()),
        ],
        compiler_params=pltpu.CompilerParams(vmem_limit_bytes=32 * 2**20),
        cost_estimate=pl.CostEstimate(
            flops=2 * 128 * HIDDEN * 7168, bytes_accessed=HIDDEN * 7168 * 4, transcendentals=0
        ),
    )(weights, lhs, fac)
    return new, nxt


def solution(mesh):
    in_specs = (P("group", "shard", None), P("group", None, None))
    out_specs = (P("group", "shard", None), P("group", None, None))
    return jax.shard_map(body, mesh=mesh, in_specs=in_specs, out_specs=out_specs, check_vma=False)
```

time: 92.2 us -> 82.4 us (0.89)
  Pallas kernels: 87.1 us -> 80.5 us
  local copies, waits for them, and re-layouts: 4.22 us -> 1.17 us
    pallas_call x1, Pallas kernels: 82 us -> 77.8 us  [body(): pl.pallas_call(main_kernel, name='rounds', out_shape=(jax.ShapeDtypeStruc...]
    unnamed x6 -> x4, local copies, waits for them, and re-layouts: 4.22 us -> 1.17 us
    pallas_call x1, Pallas kernels: 5.05 us -> 2.68 us  [body(): pl.pallas_call(update_kernel, name='update', out_shape=(jax.ShapeDtypeStr...]
where the time goes in v3:
time: 82.4 us; the launch traced here: 82.3 us
  Pallas kernels  80.5 us (98%)
  local copies, waits for them, and re-layouts  1.17 us (1%)
    pallas_call x1, Pallas kernels, body(): pl.pallas_call(main_kernel, name='rounds', out_shape=(jax.ShapeDtypeStruc...  77.8 us
    pallas_call x1, Pallas kernels, body(): pl.pallas_call(update_kernel, name='update', out_shape=(jax.ShapeDtypeStr...  2.68 us

profile of v3, /device:TPU:1, one launch (start us, length us, event | category | flops | bytes accessed | tf_op | source)
XLA Modules:
  0.0 82.3 jit_solution(11385745941835907954)
XLA Ops:
  0.6 0.0 copy-start
  0.6 0.0 copy-start.1
  0.6 1.2 %copy-done.1 = f32[1,16,7168]{2,1,0:T(8,128)S(1)} copy-done((f32[1,16,7168]{2,1,0:T(8,128)S(1)}, f32[1,16,7168]{2,1,0:T(8,128)}, u32[]{:S(2)}) %copy-start.1) | copy-done | bytes 458776
  1.8 77.8 %rounds.1 = (bf16[320,128]{1,0:T(8,128)(2,1)S(1)}, bf16[2,8,2,2,2,16,128]{6,5,4,3,2,1,0:T(8,128)(2,1)S(1)}) custom-call(bf16[320,7168]{1,0:T(8,128)(2,1)} %bitcast.2, f32[16,7168]{1,0:T(8,128)S(1)} %bitcast.3), custom_call_target="tpu_custom_call" | custom-call | flops 734003200 | bytes 4587520 | tf_op jit(solution)/shard_map/rounds/pallas_call | solution.py:320
  79.6 0.0 copy-done
  79.6 2.7 %update.1 = (bf16[1,320,7168]{2,1,0:T(8,128)(2,1)}, f32[1,16,7168]{2,1,0:T(8,128)}) custom-call(bf16[1,320,7168]{2,1,0:T(8,128)(2,1)S(1)} %copy-done, bf16[320,128]{1,0:T(8,128)(2,1)S(1)} %get-tuple-element.4.lhs_ref, bf16[2,8,2,2,2,16,128]{6,5,4,3,2,1,0:T(8,128)(2,1)S(1)} %get-tuple-element.5.fac_ref), custom_call_target="tpu_custom_call" | custom-call | flops 587202560 | bytes 9175040 | tf_op jit(solution)/shard_map/update/pallas_call | solution.py:365
Async XLA Ops:
  0.6 79.0 %copy-start = (bf16[1,320,7168]{2,1,0:T(8,128)(2,1)S(1)}, bf16[1,320,7168]{2,1,0:T(8,128)(2,1)}, u32[]{:S(2)}) copy-start(bf16[1,320,7168]{2,1,0:T(8,128)(2,1)} %w_ref.1) | copy-start | bytes 13762564
  0.6 1.2 %copy-start.1 = (f32[1,16,7168]{2,1,0:T(8,128)S(1)}, f32[1,16,7168]{2,1,0:T(8,128)}, u32[]{:S(2)}) copy-start(f32[1,16,7168]{2,1,0:T(8,128)} %param.3) | copy-start | bytes 1376260

commit v4 on v3

--- a/solution.py
+++ b/solution.py
@@ -1,5 +1,3 @@
-import functools
-
 import jax
 import jax.numpy as jnp
 from jax import lax
@@ -25,8 +23,7 @@
 
 ORDER = (4, 3, 5, 2, 6, 1, 7, 0)
 NEAR = (0, 1, 7, 2, 6, 3, 5, 4)
-GRAM_AT = 1
-GRAM_ON = 2
+GRAM_AT = 7
 ALL = tuple((d, e) for d in ORDER for e in (1, 0))
 PEERS = tuple((d, e) for d in ORDER for e in (1, 0) if d or e)
 
@@ -71,9 +68,9 @@
 
 def main_kernel(
     w_hbm, f0, lhs_ref, fac_ref,
-    w, f, xs, xc, xr, gs, gx, gz, pk, ps, pr, dd, r, bt,
-    hop, w_sem, wx_s, wx_r, init_s, init_r, c_s, c_r, x_s, x_r, gx_s, gx_r, gz_s, gz_r,
-    p_s, p_r, r_s, r_r, az_s, az_r, ag_s, ag_r, ac_s, ac_r,
+    w, f, xs, xc, xr, gs, gz, ko, kx, sn, rn, dd, r, bt,
+    hop, w_sem, wx_s, wx_r, init_s, init_r, c_s, c_r, x_s, x_r, gz_s, gz_r,
+    k_s, k_r, p_s, p_r, r_s, r_r, az_s, az_r, ax_s, ax_r, ag_s, ag_r, ac_s, ac_r,
 ):
     g = lax.axis_index("group")
     s = lax.axis_index("shard")
@@ -93,6 +90,10 @@
         copy.start()
         started.append(copy)
         return copy
+
+    def settle():
+        while started:
+            started.pop(0).wait_send()
 
     def columns(b, core):
         return pl.ds(pl.multiple_of(b * BLOCK + core * SKEW, TILE), PART)
@@ -139,6 +140,9 @@
             pl.semaphore_wait(hop.at[k, way], 1)
 
     tell(0)
+    for k in range(2):
+        hear(k)
+        tell(k + 1)
     gathers = {}
     for step in range(STEPS):
         part = jnp.zeros((2 * RANK, BOTH), F32)
@@ -146,8 +150,8 @@
             if step == 0:
                 b = i
                 if i == 4:
-                    hear(0)
-                    tell(1)
+                    hear(2)
+                    tell(3)
                 loads[b].wait()
                 swaps[b].wait_recv()
                 if b % 2 == 0:
@@ -155,9 +159,8 @@
                         copy.wait_recv()
             else:
                 b = (z + ZS - d) % ZS
-                for e in range(2):
-                    for copy in gathers[d, e]:
-                        copy.wait_recv()
+                for copy in gathers[d]:
+                    copy.wait_recv()
             tiles = []
             for t in range(4):
                 k = t // 2
@@ -171,9 +174,6 @@
             )
         xs[step, 0] = part[:RANK]
         xs[step, 1] = part[RANK:]
-        if step == 0:
-            hear(1)
-            tell(2)
         swapped = [
             send(xs.at[step, side], xr.at[step, far, 1 - side], x_s.at[step, far, side], x_r.at[step, far, 1 - side], to)
             for side, same in ((1, right), (0, left))
@@ -187,67 +187,58 @@
             (part[RANK:] + xc[step, 1]) - (xr[step, 0, 1] + xr[step, 1, 1]),
         ], axis=0)
 
-        if step == 0:
-            hear(2)
-            tell(3)
-
         stacked = jnp.concatenate(split3(raw), axis=0)
         cross_copies = []
         for i, d in enumerate(ORDER):
             b = (z + d) % ZS
             prod = jnp.dot(stacked, w[b].reshape(BOTH, PART), preferred_element_type=F32)
             prod = prod[: 2 * RANK] + (prod[2 * RANK : 4 * RANK] + prod[4 * RANK :])
-            half = PART // 2
-            ps[step, i, 0] = prod[:RANK, :half]
-            ps[step, i, 1] = prod[RANK:, half:]
-            pk[step, i, 0] = prod[:RANK, half:]
-            pk[step, i, 1] = prod[RANK:, :half]
-            cross_copies.append((
-                send(ps.at[step, i, 1], pr.at[step, i, 0], p_s.at[step, i, 1], p_r.at[step, i, 0], right),
-                send(ps.at[step, i, 0], pr.at[step, i, 1], p_s.at[step, i, 0], p_r.at[step, i, 1], left),
-            ))
+            for t in range(2):
+                own, over = slice(t * TILE, (t + 1) * TILE), slice((2 + t) * TILE, (3 + t) * TILE)
+                ko[step, i, t, 0] = -prod[:RANK, over]
+                ko[step, i, t, 1] = prod[RANK:, own]
+                sn[step, i, 0, t] = -prod[:RANK, own]
+                sn[step, i, 1, t] = prod[RANK:, over]
+            cross_copies.append([
+                send(ko.at[step, i, 1 - xh], kx.at[step, i], k_s.at[step, i], k_r.at[step, i], peer(0, 1))
+            ] + [
+                send(
+                    sn.at[step, i, side, (xh + far) % 2], rn.at[step, i, far, 1 - side],
+                    p_s.at[step, i, far, side], p_r.at[step, i, far, 1 - side], to,
+                )
+                for far, pair in ((0, (left, right)), (1, aside))
+                for side, to in enumerate(pair)
+            ])
             if i == GRAM_AT:
+                if step == 0:
+                    hear(3)
                 square = lax.dot_general(
                     raw, raw, (((1,), (1,)), ((), ())),
                     precision=lax.Precision.HIGHEST, preferred_element_type=F32,
                 )
                 gram = pack_gram(square)
                 gs[step, 0] = gram
-                gram_x = send(gs.at[step, 0], gx.at[step], gx_s.at[step], gx_r.at[step], peer(0, 1))
+                gram_copies = [
+                    send(gs.at[step, 0], gz.at[step, j], gz_s.at[step, j], gz_r.at[step, j], peer(d2, e2))
+                    for j, (d2, e2) in enumerate(PEERS)
+                ]
 
         reduce_copies = []
         for i, d in enumerate(ORDER):
-            if i == 0 and step == 0:
-                hear(3)
-            if i == GRAM_ON:
-                gram_x.wait_recv()
-                gram = gram + gx[step]
-                gs[step, 1] = gram
-                gram_copies = [
-                    send(gs.at[step, 1], gz.at[step, j], gz_s.at[step, j], gz_r.at[step, j], peer(d2, 0))
-                    for j, d2 in enumerate(ORDER[:-1])
-                ]
             for copy in cross_copies[i]:
                 copy.wait_recv()
-            diff_left = pr[step, i, 0] - pk[step, i, 0]
-            diff_right = pk[step, i, 1] - pr[step, i, 1]
-            for t in range(2):
-                dd[step, i, t, 0] = diff_left[:, t * TILE : (t + 1) * TILE]
-                dd[step, i, t, 1] = diff_right[:, t * TILE : (t + 1) * TILE]
-            for e in (1, 0):
-                if d or e:
-                    j = len(reduce_copies)
-                    reduce_copies.append(send(
-                        dd.at[step, i, (xh + e) % 2], r.at[step, j],
-                        r_s.at[step, j], r_r.at[step, j], peer(d, e),
-                    ))
+            dd[step, i] = ko[step, i, xh] + kx[step, i] + (rn[step, i, 0] + rn[step, i, 1])
+            if d:
+                reduce_copies.append(send(
+                    dd.at[step, i], r.at[step, i], r_s.at[step, i], r_r.at[step, i], peer(d, 0)
+                ))
 
         for j, copy in enumerate(gram_copies):
             copy.wait_recv()
             gram = gram + gz[step, j]
         inverses = inverse_factors(gram)
 
-        total = dd[step, ZS - 1, xh]
+        total = dd[step, ZS - 1]
         for j, copy in enumerate(reduce_copies):
             copy.wait_recv()
             total = total + r[step, j]
@@ -255,18 +246,14 @@
         f[step + 1, z, 0, xh, 0] = apply_lower(inverses[0], total[0]).astype(BF)
         f[step + 1, z, 0, xh, 1] = apply_lower(inverses[1], total[1]).astype(BF)
         piece = f.at[step + 1, z, 0, xh]
-        gathers = {}
-        for j, (d, e) in enumerate(ALL):
-            shard = peer(d, e)[1]
-            gathers[d, e] = [
-                send(
-                    piece.at[side], f.at[step + 1, z, 1, xh, 1 - side],
-                    ag_s.at[step, j, side], ag_r.at[step, j, 1 - side], (group, shard),
-                )
-                for side, group in ((1, (g + 1) % 8), (0, (g + 7) % 8))
-            ]
-            if d or e:
-                gathers[d, e].append(send(piece, piece, az_s.at[step, j], az_r.at[step, j], (g, shard)))
+        early = len(started)
+        along = {
+            d: send(piece, piece, az_s.at[step, j], az_r.at[step, j], peer(d, 0))
+            for j, d in enumerate(ORDER[:-1])
+        }
+        for copy in started[:early]:
+            copy.wait_send()
+        del started[:early]
         if step == STEPS - 1:
             basis = gossip_rate * jnp.concatenate(
                 [-apply_lower(inverses[0], raw[:RANK]), apply_lower(inverses[1], raw[RANK:])], axis=0
@@ -274,19 +261,31 @@
             terms = [term.astype(F32) for term in split3(basis)]
             bt[...] = jnp.concatenate(terms + [jnp.zeros((2 * RANK, BOTH), F32)], axis=0).T
             lhs_ref[...] = bt[pl.ds(pl.multiple_of(c * HIDDEN, 16), HIDDEN), :].astype(BF)
+        gathers = {}
+        for i, d in enumerate(NEAR):
+            if d:
+                along[d].wait_recv()
+            b = (z + ZS - d) % ZS
+            here = f.at[step + 1, b, 0, xh]
+            gathers[d] = [send(here, here, ax_s.at[step, i], ax_r.at[step, i], peer(0, 1))] + [
+                send(
+                    here.at[side], f.at[step + 1, b, 1, xh, 1 - side],
+                    ag_s.at[step, i, far, side], ag_r.at[step, i, far, 1 - side], to,
+                )
+                for far, pair in ((1, aside), (0, (left, right)))
+                for side, to in enumerate(pair)
+            ]
 
     lasts = []
     for i, d in enumerate(NEAR):
         b = (z + ZS - d) % ZS
-        for e in range(2):
-            for copy in gathers[d, e]:
-                copy.wait_recv()
+        for copy in gathers[d]:
+            copy.wait_recv()
         lasts.append(send(f.at[STEPS, b], fac_ref.at[c, b], ac_s.at[i], ac_r.at[i], other))
         fac_ref[c, b] = f[STEPS, b]
+    settle()
     for copy in lasts:
         copy.wait_recv()
-    for copy in started:
-        copy.wait_send()
 
 
 def update_kernel(w_ref, lhs_ref, fac_ref, new_hbm, next_hbm, new, nxt, new_sem, next_sem):
@@ -333,13 +332,13 @@
             pltpu.VMEM((STEPS, 2, RANK, BOTH), F32),
             pltpu.VMEM((STEPS, 2, 2, RANK, BOTH), F32),
             pltpu.VMEM((STEPS, 2, 8, TILE), F32),
-            pltpu.VMEM((STEPS, 8, TILE), F32),
-            pltpu.VMEM((STEPS, ZS - 1, 8, TILE), F32),
-            pltpu.VMEM((STEPS, ZS, 2, RANK, PART // 2), F32),
-            pltpu.VMEM((STEPS, ZS, 2, RANK, PART // 2), F32),
-            pltpu.VMEM((STEPS, ZS, 2, RANK, PART // 2), F32),
+            pltpu.VMEM((STEPS, n, 8, TILE), F32),
             pltpu.VMEM((STEPS, ZS, 2, 2, RANK, TILE), F32),
-            pltpu.VMEM((STEPS, n, 2, RANK, TILE), F32),
+            pltpu.VMEM((STEPS, ZS, 2, RANK, TILE), F32),
+            pltpu.VMEM((STEPS, ZS, 2, 2, RANK, TILE), F32),
+            pltpu.VMEM((STEPS, ZS, 2, 2, RANK, TILE), F32),
+            pltpu.VMEM((STEPS, ZS, 2, RANK, TILE), F32),
+            pltpu.VMEM((STEPS, ZS - 1, 2, RANK, TILE), F32),
             pltpu.VMEM((BOTH, TILE), F32),
             pltpu.SemaphoreType.REGULAR((4, 2)),
             dma((ZS,)),
@@ -347,12 +346,13 @@
             dma((ZS // 2, 2)), dma((ZS // 2, 2)),
             dma((STEPS,)), dma((STEPS,)),
             dma((STEPS, 2, 2)), dma((STEPS, 2, 2)),
-            dma((STEPS,)), dma((STEPS,)),
+            dma((STEPS, n)), dma((STEPS, n)),
+            dma((STEPS, ZS)), dma((STEPS, ZS)),
+            dma((STEPS, ZS, 2, 2)), dma((STEPS, ZS, 2, 2)),
             dma((STEPS, ZS - 1)), dma((STEPS, ZS - 1)),
-            dma((STEPS, ZS, 2)), dma((STEPS, ZS, 2)),
-            dma((STEPS, n)), dma((STEPS, n)),
-            dma((STEPS, n + 1)), dma((STEPS, n + 1)),
-            dma((STEPS, n + 1, 2)), dma((STEPS, n + 1, 2)),
+            dma((STEPS, ZS - 1)), dma((STEPS, ZS - 1)),
+            dma((STEPS, ZS)), dma((STEPS, ZS)),
+            dma((STEPS, ZS, 2, 2)), dma((STEPS, ZS, 2, 2)),
             dma((ZS,)), dma((ZS,)),
         ],
         compiler_params=pltpu.CompilerParams(

time: 82.4 us -> 78.9 us (0.958)
  Pallas kernels: 80.5 us -> 77 us
    pallas_call x1, Pallas kernels: 77.8 us -> 74.3 us  [body(): pl.pallas_call(main_kernel, name='rounds', out_shape=(jax.ShapeDtypeStruc...]
where the time goes in v4:
time: 78.9 us; the launch traced here: 78.8 us
  Pallas kernels  77 us (98%)
  local copies, waits for them, and re-layouts  1.17 us (1%)
    pallas_call x1, Pallas kernels, body(): pl.pallas_call(main_kernel, name='rounds', out_shape=(jax.ShapeDtypeStruc...  74.3 us
    pallas_call x1, Pallas kernels, body(): pl.pallas_call(update_kernel, name='update', out_shape=(jax.ShapeDtypeStr...  2.68 us

profile of v4, /device:TPU:1, one launch (start us, length us, event | category | flops | bytes accessed | tf_op | source)
XLA Modules:
  0.0 78.8 jit_solution(12772748243785844653)
XLA Ops:
  0.6 0.0 copy-start
  0.6 0.0 copy-start.1
  0.6 1.2 %copy-done.1 = f32[1,16,7168]{2,1,0:T(8,128)S(1)} copy-done((f32[1,16,7168]{2,1,0:T(8,128)S(1)}, f32[1,16,7168]{2,1,0:T(8,128)}, u32[]{:S(2)}) %copy-start.1) | copy-done | bytes 458776
  1.8 74.3 %rounds.1 = (bf16[320,128]{1,0:T(8,128)(2,1)S(1)}, bf16[2,8,2,2,2,16,128]{6,5,4,3,2,1,0:T(8,128)(2,1)S(1)}) custom-call(bf16[320,7168]{1,0:T(8,128)(2,1)} %bitcast.2, f32[16,7168]{1,0:T(8,128)S(1)} %bitcast.3), custom_call_target="tpu_custom_call" | custom-call | flops 734003200 | bytes 4587520 | tf_op jit(solution)/shard_map/rounds/pallas_call | solution.py:319
  76.1 0.0 copy-done
  76.2 2.7 %update.1 = (bf16[1,320,7168]{2,1,0:T(8,128)(2,1)}, f32[1,16,7168]{2,1,0:T(8,128)}) custom-call(bf16[1,320,7168]{2,1,0:T(8,128)(2,1)S(1)} %copy-done, bf16[320,128]{1,0:T(8,128)(2,1)S(1)} %get-tuple-element.4.lhs_ref, bf16[2,8,2,2,2,16,128]{6,5,4,3,2,1,0:T(8,128)(2,1)S(1)} %get-tuple-element.5.fac_ref), custom_call_target="tpu_custom_call" | custom-call | flops 587202560 | bytes 9175040 | tf_op jit(solution)/shard_map/update/pallas_call | solution.py:365
Async XLA Ops:
  0.6 75.5 %copy-start = (bf16[1,320,7168]{2,1,0:T(8,128)(2,1)S(1)}, bf16[1,320,7168]{2,1,0:T(8,128)(2,1)}, u32[]{:S(2)}) copy-start(bf16[1,320,7168]{2,1,0:T(8,128)(2,1)} %w_ref.1) | copy-start | bytes 13762564
  0.6 1.2 %copy-start.1 = (f32[1,16,7168]{2,1,0:T(8,128)S(1)}, f32[1,16,7168]{2,1,0:T(8,128)}, u32[]{:S(2)}) copy-start(f32[1,16,7168]{2,1,0:T(8,128)} %param.3) | copy-start | bytes 1376260

commit v5 on v4

--- a/solution.py
+++ b/solution.py
@@ -67,9 +67,9 @@
 
 
 def main_kernel(
-    w_hbm, f0, lhs_ref, fac_ref,
-    w, f, xs, xc, xr, gs, gz, ko, kx, sn, rn, dd, r, bt,
-    hop, w_sem, wx_s, wx_r, init_s, init_r, c_s, c_r, x_s, x_r, gz_s, gz_r,
+    w_hbm, f0_hbm, lhs_ref, fac_ref,
+    w, f0, f, xs, xc, xr, gs, gz, ko, kx, sn, rn, dd, r, bt,
+    hop, w_sem, f0_sem, wx_s, wx_r, init_s, init_r, c_s, c_r, x_s, x_r, gz_s, gz_r,
     k_s, k_r, p_s, p_r, r_s, r_r, az_s, az_r, ax_s, ax_r, ag_s, ag_r, ac_s, ac_r,
 ):
     g = lax.axis_index("group")
@@ -99,6 +99,8 @@
         return pl.ds(pl.multiple_of(b * BLOCK + core * SKEW, TILE), PART)
 
     beyond = [((g + k) % 8, s + 1 - 2 * c) for k in (7, 1)]
+    f0_load = pltpu.make_async_copy(f0_hbm, f0, f0_sem)
+    f0_load.start()
     barrier = pltpu.get_barrier_semaphore()
     above, below = peer(1, 0), peer(7, 0)
     aside = [((g + k) % 8, peer(0, 1)[1]) for k in (7, 1)]
@@ -112,16 +114,30 @@
         load.start()
         loads.append(load)
 
+    def tell(k):
+        for way, device in enumerate((above, below)):
+            pl.semaphore_signal(hop.at[k, way], inc=1, device_id=device, device_id_type=MESH)
+
+    def hear(k):
+        for way in range(2):
+            pl.semaphore_wait(hop.at[k, way], 1)
+
+    pl.semaphore_wait(barrier, len(greeted))
+    tell(0)
+
+    swaps = [
+        send(w_hbm.at[:, columns(b, 1 - c)], w.at[b, c], wx_s.at[b], wx_r.at[b], other)
+        for b in range(ZS)
+    ]
+
+    f0_load.wait()
+    first = []
     for b in range(ZS):
         for t in range(4):
             tile = pl.ds(pl.multiple_of(b * BLOCK + c * SKEW + t * TILE, TILE), TILE)
             f[0, b, t // 2, t % 2, 1] = f0[:, tile].astype(BF)
-    pl.semaphore_wait(barrier, len(greeted))
-
-    first, swaps = [], []
-    for b in range(ZS):
-        if b % 2 == 0:
-            two = pl.ds(b, 2)
+        if b % 2:
+            two = pl.ds(b - 1, 2)
             first.append([
                 send(
                     f.at[0, two, k, :, 1], f.at[0, two, 1 - k, :, 0],
@@ -129,17 +145,7 @@
                 )
                 for k in range(2)
             ])
-        swaps.append(send(w_hbm.at[:, columns(b, 1 - c)], w.at[b, c], wx_s.at[b], wx_r.at[b], other))
-
-    def tell(k):
-        for way, device in enumerate((above, below)):
-            pl.semaphore_signal(hop.at[k, way], inc=1, device_id=device, device_id_type=MESH)
-
-    def hear(k):
-        for way in range(2):
-            pl.semaphore_wait(hop.at[k, way], 1)
-
-    tell(0)
+
     for k in range(2):
         hear(k)
         tell(k + 1)
@@ -323,10 +329,11 @@
             jax.ShapeDtypeStruct((HIDDEN, TILE), BF),
             jax.ShapeDtypeStruct((2, ZS, 2, 2, 2, RANK, TILE), BF),
         ),
-        in_specs=[pl.BlockSpec(memory_space=pltpu.HBM), pl.BlockSpec(memory_space=pltpu.VMEM)],
+        in_specs=[pl.BlockSpec(memory_space=pltpu.HBM)] * 2,
         out_specs=[pl.BlockSpec(memory_space=pltpu.VMEM)] * 2,
         scratch_shapes=[
             pltpu.VMEM((ZS, 2, HIDDEN, PART), BF),
+            pltpu.VMEM((RANK, ZS * BLOCK), F32),
             pltpu.VMEM((STEPS + 1, ZS, 2, 2, 2, RANK, TILE), BF),
             pltpu.VMEM((STEPS, 2, RANK, BOTH), F32),
             pltpu.VMEM((STEPS, 2, RANK, BOTH), F32),
@@ -341,7 +348,7 @@
             pltpu.VMEM((STEPS, ZS - 1, 2, RANK, TILE), F32),
             pltpu.VMEM((BOTH, TILE), F32),
             pltpu.SemaphoreType.REGULAR((4, 2)),
-            dma((ZS,)),
+            dma((ZS,)), dma(()),
             dma((ZS,)), dma((ZS,)),
             dma((ZS // 2, 2)), dma((ZS // 2, 2)),
             dma((STEPS,)), dma((STEPS,)),
@@ -361,7 +368,7 @@
         cost_estimate=pl.CostEstimate(
             flops=10 * 32 * HIDDEN * 7168, bytes_accessed=HIDDEN * 7168 * 2, transcendentals=0
         ),
-    )(weights[0], factor_init[0])
+    )(*(pltpu.with_memory_space_constraint(x, pltpu.HBM) for x in (weights[0], factor_init[0])))
     new, nxt = pl.pallas_call(
         update_kernel,
         name="update",

time: 78.9 us -> 78 us (0.989)
  local copies, waits for them, and re-layouts: 1.17 us -> 0.01 us
    unnamed x4 -> x2, local copies, waits for them, and re-layouts: 1.17 us -> 0.01 us
where the time goes in v5:
time: 78 us; the launch traced here: 77.9 us
  Pallas kernels  77.2 us (99%)
    pallas_call x1, Pallas kernels, body(): pl.pallas_call(main_kernel, name='rounds', out_shape=(jax.ShapeDtypeStruc...  74.6 us
    pallas_call x1, Pallas kernels, body(): pl.pallas_call(update_kernel, name='update', out_shape=(jax.ShapeDtypeStr...  2.68 us

profile of v5, /device:TPU:1, one launch (start us, length us, event | category | flops | bytes accessed | tf_op | source)
XLA Modules:
  0.0 77.9 jit_solution(9820357554838566103)
XLA Ops:
  0.6 0.0 copy-start
  0.6 74.6 %rounds.1 = (bf16[320,128]{1,0:T(8,128)(2,1)S(1)}, bf16[2,8,2,2,2,16,128]{6,5,4,3,2,1,0:T(8,128)(2,1)S(1)}) custom-call(bf16[320,7168]{1,0:T(8,128)(2,1)} %bitcast.2, f32[16,7168]{1,0:T(8,128)} %bitcast.3), custom_call_target="tpu_custom_call" | custom-call | flops 734003200 | bytes 4587520 | tf_op jit(solution)/shard_map/rounds/pallas_call | solution.py:325
  75.2 0.0 copy-done
  75.2 2.7 %update.1 = (bf16[1,320,7168]{2,1,0:T(8,128)(2,1)}, f32[1,16,7168]{2,1,0:T(8,128)}) custom-call(bf16[1,320,7168]{2,1,0:T(8,128)(2,1)S(1)} %copy-done, bf16[320,128]{1,0:T(8,128)(2,1)S(1)} %get-tuple-element.4.lhs_ref, bf16[2,8,2,2,2,16,128]{6,5,4,3,2,1,0:T(8,128)(2,1)S(1)} %get-tuple-element.5.fac_ref), custom_call_target="tpu_custom_call" | custom-call | flops 587202560 | bytes 9175040 | tf_op jit(solution)/shard_map/update/pallas_call | solution.py:372
Async XLA Ops:
  0.6 74.6 %copy-start = (bf16[1,320,7168]{2,1,0:T(8,128)(2,1)S(1)}, bf16[1,320,7168]{2,1,0:T(8,128)(2,1)}, u32[]{:S(2)}) copy-start(bf16[1,320,7168]{2,1,0:T(8,128)(2,1)} %w_ref.1) | copy-start | bytes 13762564

commit v6 on v5

--- a/solution.py
+++ b/solution.py
@@ -23,7 +23,8 @@
 
 ORDER = (4, 3, 5, 2, 6, 1, 7, 0)
 NEAR = (0, 1, 7, 2, 6, 3, 5, 4)
-GRAM_AT = 7
+GRAM_ON = 1
+GRAM_AT = 2
 ALL = tuple((d, e) for d in ORDER for e in (1, 0))
 PEERS = tuple((d, e) for d in ORDER for e in (1, 0) if d or e)
 
@@ -68,8 +69,8 @@
 
 def main_kernel(
     w_hbm, f0_hbm, lhs_ref, fac_ref,
-    w, f0, f, xs, xc, xr, gs, gz, ko, kx, sn, rn, dd, r, bt,
-    hop, w_sem, f0_sem, wx_s, wx_r, init_s, init_r, c_s, c_r, x_s, x_r, gz_s, gz_r,
+    w, f0, f, xs, xc, xr, gs, gx, gz, ko, kx, sn, rn, dd, r, bt,
+    hop, w_sem, f0_sem, wx_s, wx_r, init_s, init_r, c_s, c_r, x_s, x_r, gx_s, gx_r, gz_s, gz_r,
     k_s, k_r, p_s, p_r, r_s, r_r, az_s, az_r, ax_s, ax_r, ag_s, ag_r, ac_s, ac_r,
 ):
     g = lax.axis_index("group")
@@ -224,13 +225,18 @@
                 )
                 gram = pack_gram(square)
                 gs[step, 0] = gram
-                gram_copies = [
-                    send(gs.at[step, 0], gz.at[step, j], gz_s.at[step, j], gz_r.at[step, j], peer(d2, e2))
-                    for j, (d2, e2) in enumerate(PEERS)
-                ]
+                gram_x = send(gs.at[step, 0], gx.at[step], gx_s.at[step], gx_r.at[step], peer(0, 1))
 
         reduce_copies = []
         for i, d in enumerate(ORDER):
+            if i == GRAM_ON:
+                gram_x.wait_recv()
+                gram = gram + gx[step]
+                gs[step, 1] = gram
+                gram_copies = [
+                    send(gs.at[step, 1], gz.at[step, j], gz_s.at[step, j], gz_r.at[step, j], peer(d2, 0))
+                    for j, d2 in enumerate(ORDER[:-1])
+                ]
             for copy in cross_copies[i]:
                 copy.wait_recv()
             dd[step, i] = ko[step, i, xh] + kx[step, i] + (rn[step, i, 0] + rn[step, i, 1])
@@ -273,14 +279,14 @@
                 along[d].wait_recv()
             b = (z + ZS - d) % ZS
             here = f.at[step + 1, b, 0, xh]
-            gathers[d] = [send(here, here, ax_s.at[step, i], ax_r.at[step, i], peer(0, 1))] + [
+            gathers[d] = [
                 send(
                     here.at[side], f.at[step + 1, b, 1, xh, 1 - side],
                     ag_s.at[step, i, far, side], ag_r.at[step, i, far, 1 - side], to,
                 )
-                for far, pair in ((1, aside), (0, (left, right)))
+                for far, pair in ((0, (left, right)), (1, aside))
                 for side, to in enumerate(pair)
-            ]
+            ] + [send(here, here, ax_s.at[step, i], ax_r.at[step, i], peer(0, 1))]
 
     lasts = []
     for i, d in enumerate(NEAR):
@@ -339,7 +345,8 @@
             pltpu.VMEM((STEPS, 2, RANK, BOTH), F32),
             pltpu.VMEM((STEPS, 2, 2, RANK, BOTH), F32),
             pltpu.VMEM((STEPS, 2, 8, TILE), F32),
-            pltpu.VMEM((STEPS, n, 8, TILE), F32),
+            pltpu.VMEM((STEPS, 8, TILE), F32),
+            pltpu.VMEM((STEPS, ZS - 1, 8, TILE), F32),
             pltpu.VMEM((STEPS, ZS, 2, 2, RANK, TILE), F32),
             pltpu.VMEM((STEPS, ZS, 2, RANK, TILE), F32),
             pltpu.VMEM((STEPS, ZS, 2, 2, RANK, TILE), F32),
@@ -353,7 +360,8 @@
             dma((ZS // 2, 2)), dma((ZS // 2, 2)),
             dma((STEPS,)), dma((STEPS,)),
             dma((STEPS, 2, 2)), dma((STEPS, 2, 2)),
-            dma((STEPS, n)), dma((STEPS, n)),
+            dma((STEPS,)), dma((STEPS,)),
+            dma((STEPS, ZS - 1)), dma((STEPS, ZS - 1)),
             dma((STEPS, ZS)), dma((STEPS, ZS)),
             dma((STEPS, ZS, 2, 2)), dma((STEPS, ZS, 2, 2)),
             dma((STEPS, ZS - 1)), dma((STEPS, ZS - 1)),

time: 78 us -> 77 us (0.987)
  Pallas kernels: 77.2 us -> 76.3 us
    pallas_call x1, Pallas kernels: 74.6 us -> 73.6 us  [body(): pl.pallas_call(main_kernel, name='rounds', out_shape=(jax.ShapeDtypeStruc...]
where the time goes in v6:
time: 77 us; the launch traced here: 76.9 us
  Pallas kernels  76.3 us (99%)
    pallas_call x1, Pallas kernels, body(): pl.pallas_call(main_kernel, name='rounds', out_shape=(jax.ShapeDtypeStruc...  73.6 us
    pallas_call x1, Pallas kernels, body(): pl.pallas_call(update_kernel, name='update', out_shape=(jax.ShapeDtypeStr...  2.68 us

profile of v6, /device:TPU:1, one launch (start us, length us, event | category | flops | bytes accessed | tf_op | source)
XLA Modules:
  0.0 76.9 jit_solution(11966875826190230850)
XLA Ops:
  0.6 0.0 copy-start
  0.6 73.6 %rounds.1 = (bf16[320,128]{1,0:T(8,128)(2,1)S(1)}, bf16[2,8,2,2,2,16,128]{6,5,4,3,2,1,0:T(8,128)(2,1)S(1)}) custom-call(bf16[320,7168]{1,0:T(8,128)(2,1)} %bitcast.2, f32[16,7168]{1,0:T(8,128)} %bitcast.3), custom_call_target="tpu_custom_call" | custom-call | flops 734003200 | bytes 4587520 | tf_op jit(solution)/shard_map/rounds/pallas_call | solution.py:331
  74.3 0.0 copy-done
  74.3 2.7 %update.1 = (bf16[1,320,7168]{2,1,0:T(8,128)(2,1)}, f32[1,16,7168]{2,1,0:T(8,128)}) custom-call(bf16[1,320,7168]{2,1,0:T(8,128)(2,1)S(1)} %copy-done, bf16[320,128]{1,0:T(8,128)(2,1)S(1)} %get-tuple-element.4.lhs_ref, bf16[2,8,2,2,2,16,128]{6,5,4,3,2,1,0:T(8,128)(2,1)S(1)} %get-tuple-element.5.fac_ref), custom_call_target="tpu_custom_call" | custom-call | flops 587202560 | bytes 9175040 | tf_op jit(solution)/shard_map/update/pallas_call | solution.py:380
Async XLA Ops:
  0.6 73.6 %copy-start = (bf16[1,320,7168]{2,1,0:T(8,128)(2,1)S(1)}, bf16[1,320,7168]{2,1,0:T(8,128)(2,1)}, u32[]{:S(2)}) copy-start(bf16[1,320,7168]{2,1,0:T(8,128)(2,1)} %w_ref.1) | copy-start | bytes 13762564

commit v7 on v6

--- a/solution.py
+++ b/solution.py
@@ -23,8 +23,8 @@
 
 ORDER = (4, 3, 5, 2, 6, 1, 7, 0)
 NEAR = (0, 1, 7, 2, 6, 3, 5, 4)
-GRAM_ON = 1
-GRAM_AT = 2
+GRAM_ON = 2
+GRAM_AT = 4
 ALL = tuple((d, e) for d in ORDER for e in (1, 0))
 PEERS = tuple((d, e) for d in ORDER for e in (1, 0) if d or e)
 

time: 77 us -> 79.6 us (1.034)
  Pallas kernels: 76.3 us -> 78.9 us
    pallas_call x1, Pallas kernels: 73.6 us -> 76.2 us  [body(): pl.pallas_call(main_kernel, name='rounds', out_shape=(jax.ShapeDtypeStruc...]
where the time goes in v7:
time: 79.6 us; the launch traced here: 79.5 us
  Pallas kernels  78.9 us (99%)
    pallas_call x1, Pallas kernels, body(): pl.pallas_call(main_kernel, name='rounds', out_shape=(jax.ShapeDtypeStruc...  76.2 us
    pallas_call x1, Pallas kernels, body(): pl.pallas_call(update_kernel, name='update', out_shape=(jax.ShapeDtypeStr...  2.68 us

profile of v7, /device:TPU:1, one launch (start us, length us, event | category | flops | bytes accessed | tf_op | source)
XLA Modules:
  0.0 79.5 jit_solution(13471688016781011059)
XLA Ops:
  0.6 0.0 copy-start
  0.6 76.2 %rounds.1 = (bf16[320,128]{1,0:T(8,128)(2,1)S(1)}, bf16[2,8,2,2,2,16,128]{6,5,4,3,2,1,0:T(8,128)(2,1)S(1)}) custom-call(bf16[320,7168]{1,0:T(8,128)(2,1)} %bitcast.2, f32[16,7168]{1,0:T(8,128)} %bitcast.3), custom_call_target="tpu_custom_call" | custom-call | flops 734003200 | bytes 4587520 | tf_op jit(solution)/shard_map/rounds/pallas_call | solution.py:331
  76.8 0.0 copy-done
  76.9 2.7 %update.1 = (bf16[1,320,7168]{2,1,0:T(8,128)(2,1)}, f32[1,16,7168]{2,1,0:T(8,128)}) custom-call(bf16[1,320,7168]{2,1,0:T(8,128)(2,1)S(1)} %copy-done, bf16[320,128]{1,0:T(8,128)(2,1)S(1)} %get-tuple-element.4.lhs_ref, bf16[2,8,2,2,2,16,128]{6,5,4,3,2,1,0:T(8,128)(2,1)S(1)} %get-tuple-element.5.fac_ref), custom_call_target="tpu_custom_call" | custom-call | flops 587202560 | bytes 9175040 | tf_op jit(solution)/shard_map/update/pallas_call | solution.py:380
Async XLA Ops:
  0.6 76.2 %copy-start = (bf16[1,320,7168]{2,1,0:T(8,128)(2,1)S(1)}, bf16[1,320,7168]{2,1,0:T(8,128)(2,1)}, u32[]{:S(2)}) copy-start(bf16[1,320,7168]{2,1,0:T(8,128)(2,1)} %w_ref.1) | copy-start | bytes 13762564
